TPU v7x, 256 devices: a whole 4x4x8 slice. The times are simulated.
256 devices in a mesh: seq: 64 (over z, y, x_hi), dp: 4 (over x_lo, core).
Axes of the slice: x: 4 (x_hi: 2, x_lo: 2; x = x_hi * 2 + x_lo), y: 4, z: 8, core: 2. Of those that a mesh axis runs over, the one named last changes fastest.
Arguments:
- frames: float32 [4, 64, 192, 768], P('dp', 'seq'), may hold values from -6 to 6
- out_cotangent: float32 [4, 64, 192, 768], P('dp', 'seq'), may hold values from -0.6 to 0.6
- layer_norm_gain: float32 [768], replicated, may hold values from 0.5 to 1.5
- layer_norm_bias: float32 [768], replicated, may hold values from -1.2 to 1.2
- qkv_weight: float32 [768, 2304], P('seq'), may hold values from -2 to 2
- proj_weight: float32 [768, 768], P('seq'), may hold values from -0.21875 to 0.21875
- proj_bias: float32 [768], replicated, may hold values from -1.2 to 1.2
Outputs:
- frames_out: float32 [4, 64, 192, 768], P('dp', 'seq')
- grad_frames: float32 [4, 64, 192, 768], P('dp', 'seq')
- grad_ln_gain: float32 [768], replicated
- grad_ln_bias: float32 [768], replicated
- grad_qkv_weight: float32 [768, 2304], P('seq')
- grad_proj_weight: float32 [768, 768], P('seq')
- grad_proj_bias: float32 [768], replicated
All inputs are finite; a program needn't handle non-finite values.
Results may differ from a plain program's by a relative error of at most 0.00015.
Values sent between devices are 32-bit elements; how exact they have to be, the bound alone decides.
A program may use at most 128 MiB of HBM per device.

v0:
```python
import math

import jax
import jax.numpy as jnp
from jax import lax
from jax.sharding import PartitionSpec as P

HEADS = 12


EPSILON = 1e-06


def fetch(qkv_part, proj_part):
    return (
        lax.all_gather(qkv_part, "seq", axis=0, tiled=True),
        lax.all_gather(proj_part, "seq", axis=0, tiled=True),
    )


def on_device(
    frames, out_cotangent, layer_norm_gain, layer_norm_bias, qkv_weight, proj_weight, proj_bias
):
    highest = lax.Precision.HIGHEST
    width = frames.shape[3]
    head_size = width // HEADS
    scale = 1.0 / math.sqrt(head_size)
    moved_x, moved_dy = (
        lax.all_to_all(frames, "seq", split_axis=2, concat_axis=1, tiled=True),
        lax.all_to_all(out_cotangent, "seq", split_axis=2, concat_axis=1, tiled=True),
    )
    layout = moved_x.shape
    rows_x = moved_x.reshape(-1, width)
    rows_dy = moved_dy.reshape(-1, width)
    full_qkv, full_proj = fetch(qkv_weight, proj_weight)
    row_average = jnp.mean(rows_x, axis=-1, keepdims=True)
    centered_rows = rows_x - row_average
    inverse_deviation = lax.rsqrt(
        jnp.mean(centered_rows * centered_rows, axis=-1, keepdims=True) + EPSILON
    )
    normalized_input = centered_rows * inverse_deviation
    norm_output = normalized_input * layer_norm_gain + layer_norm_bias
    qkv = jnp.dot(norm_output, full_qkv, precision=highest)
    qkv = qkv.reshape(layout[0], layout[1], layout[2], 3, HEADS, head_size)
    queries = qkv[:, :, :, 0]
    keys = qkv[:, :, :, 1]
    values = qkv[:, :, :, 2]
    scores = jnp.einsum("ctphd,cfphd->cphtf", queries, keys, precision=highest) * scale
    probs = jax.nn.softmax(scores, axis=-1)
    attended = jnp.einsum("cphtf,cfphd->ctphd", probs, values, precision=highest).reshape(-1, width)
    output = rows_x + jnp.dot(attended, full_proj, precision=highest) + proj_bias
    held = lax.optimization_barrier((qkv_weight, proj_weight, attended))
    back_qkv, back_proj = fetch(held[0], held[1])
    d_attended = jnp.einsum("rn,kn->rk", rows_dy, back_proj, precision=highest).reshape(
        queries.shape
    )
    d_probs = jnp.einsum("ctphd,cfphd->cphtf", d_attended, values, precision=highest)
    d_values = jnp.einsum("cphtf,ctphd->cfphd", probs, d_attended, precision=highest)
    d_scores = probs * (d_probs - jnp.sum(d_probs * probs, axis=-1, keepdims=True)) * scale
    d_queries = jnp.einsum("cphtf,cfphd->ctphd", d_scores, keys, precision=highest)
    d_keys = jnp.einsum("cphtf,ctphd->cfphd", d_scores, queries, precision=highest)
    d_qkv = jnp.stack([d_queries, d_keys, d_values], axis=3).reshape(-1, 3 * width)
    grad_norm_output = jnp.einsum("rn,kn->rk", d_qkv, back_qkv, precision=highest)
    gain_product = jnp.sum(grad_norm_output * normalized_input, axis=0)
    bias_term = jnp.sum(grad_norm_output, axis=0)
    proj_term = jnp.sum(rows_dy, axis=0)
    grad_normalized = grad_norm_output * layer_norm_gain
    d_rows = rows_dy + inverse_deviation * (
        grad_normalized
        - jnp.mean(grad_normalized, axis=-1, keepdims=True)
        - normalized_input * jnp.mean(grad_normalized * normalized_input, axis=-1, keepdims=True)
    )
    out_frames, grad_frames = (
        lax.all_to_all(output.reshape(layout), "seq", split_axis=1, concat_axis=2, tiled=True),
        lax.all_to_all(d_rows.reshape(layout), "seq", split_axis=1, concat_axis=2, tiled=True),
    )
    qkv_part = jnp.einsum("rk,rn->kn", norm_output, d_qkv, precision=highest)
    proj_part = jnp.einsum("rk,rn->kn", attended, rows_dy, precision=highest)
    share = lax.psum_scatter(
        jnp.concatenate([qkv_part, proj_part], axis=1), "seq", scatter_dimension=0, tiled=True
    )
    share = lax.psum(share, "dp")
    small = lax.psum((gain_product, bias_term, proj_term), ("seq", "dp"))
    return (
        out_frames,
        grad_frames,
        small[0],
        small[1],
        share[:, : 3 * width],
        share[:, 3 * width :],
        small[2],
    )


def solution(mesh):
    return jax.shard_map(
        on_device,
        mesh=mesh,
        in_specs=(
            P("dp", "seq", None, None),
            P("dp", "seq", None, None),
            P(),
            P(),
            P("seq", None),
            P("seq", None),
            P(),
        ),
        out_specs=(
            P("dp", "seq", None, None),
            P("dp", "seq", None, None),
            P(),
            P(),
            P("seq", None),
            P("seq", None),
            P(),
        ),
        check_vma=False,
    )
```

profile of v0, /device:TPU:1, one launch (start us, length us, event | category | flops | bytes accessed | tf_op | source)
XLA Modules:
  0.0 1102.9 jit_solution(884192875722742444)
XLA Ops:
  7.9 0.7 all-gather.11.cloned.1.call-update
  8.7 1.7 copy.62
  10.4 34.5 %all_to_all.42 = f32[1,1,192,768]{3,1,0,2:T(1,128)S(1)} all-to-all(f32[1,1,192,768]{3,1,0,2:T(1,128)S(1)} %copy.62), channel_id=1, replica_groups=mesh['seq'=64,'dp'=4] {'seq'}, dimensions={2} | all-to-all | bytes 1179648 | tf_op jit(solution)/shard_map/all_to_all | solution.py:29
  44.9 1.0 reduce_sum.81
  47.2 125.1 %all-gather.9.cloned.1.call-done = f32[64,12,2304]{2,1,0:T(8,128)} async-done(((f32[1,12,2304]{2,1,0:T(8,128)}), f32[64,12,2304]{2,1,0:T(8,128)}) %all-gather.9.cloned.1.call-update) | async-done | bytes 7077904 | tf_op jit(solution)/shard_map/all_gather | solution.py:16
  172.3 8.7 reshape.210
  181.0 8.0 copy.64
  189.0 11.1 %convolution_bitcast_fusion = f32[1,64,3,3,12,64]{5,1,4,3,2,0:T(8,128)S(1)} fusion(f32[3,12,64,768,1]{3,2,1,0,4:T(8,128)} %bitcast.92, f32[64,3,768,1,1]{2,1,0,4,3:T(4,128)S(1)} %bitcast.94), kind=kOutput, calls=%fused_computation.2 | convolution fusion | flops 4076863488 | bytes 9437184 | tf_op jit(solution)/shard_map/dot_general | solution.py:43
  200.1 2.0 fusion.23
  202.4 0.8 copy-done.3
  203.8 3.2 convolution_bitcast_fusion.4
  206.9 2.0 copy.68
  208.9 1.2 reshape.203
  210.2 1.4 copy.70
  211.6 7.7 all-to-all-start.2
  219.4 74.8 %all-gather.11.cloned.1.call-done = f32[64,12,768]{2,1,0:T(8,128)} async-done(((f32[1,12,768]{2,1,0:T(8,128)}), f32[64,12,768]{2,1,0:T(8,128)}) %all-gather.11.cloned.1.call-update) | async-done | bytes 2359312 | tf_op jit(solution)/shard_map/all_gather | solution.py:17
  294.2 3.8 reshape.212
  298.0 3.4 fusion.1
  301.4 1.4 reshape.219
  302.8 8.3 all-to-all-start.1
  311.2 3.5 fusion.5
  314.7 103.4 %all-gather.13.cloned.1.call-done = f32[64,12,768]{2,1,0:T(8,128)} async-done(((f32[1,12,768]{2,1,0:T(8,128)}), f32[64,12,768]{2,1,0:T(8,128)}) %all-gather.13.cloned.1.call-update) | async-done | bytes 2359312 | tf_op jit(solution)/shard_map/all_gather | solution.py:17
  418.1 4.0 reshape.214
  422.1 5.0 convolution_bitcast_fusion.5
  427.2 1.4 reshape.206
  428.6 1.5 copy.76
  430.1 3.6 multiply_reduce_fusion
  433.8 2.4 convolution_bitcast_fusion.2
  436.1 2.4 convolution_bitcast_fusion.3
  438.6 2.2 convolution_bitcast_fusion.1
  440.7 2.1 pad_maximum_fusion.1
  442.8 6.3 copy.78
  449.1 3.6 reshape.207
  452.8 7.9 fusion.8
  460.6 8.8 pad_maximum_fusion
  469.4 317.4 %fusion = f32[16,3072]{1,0:T(8,128)S(1)} fusion(f32[768,3072]{1,0:T(8,128)} %pad_maximum_fusion), kind=kCustom, calls=%all-reduce-scatter | all-reduce-scatter fusion | flops 3145729 | bytes 9634816
  786.8 1.7 collective-permute-start.15
  788.6 8.7 reshape.216
  797.3 10.1 multiply_reduce_fusion.1
  807.7 1.4 reshape.220
  809.1 9.6 all-to-all-start.3
  818.8 7.4 collective-permute-start.14
  826.3 4.4 collective-permute-start.13
  830.6 4.4 collective-permute-start.12
  835.0 4.4 collective-permute-start.11
  839.4 2.5 collective-permute-start.10
  841.9 5.3 collective-permute-start.9
  847.2 1.3 collective-permute-start.8
  848.6 17.7 %collective-permute-start.7 = (f32[16,3072]{1,0:T(8,128)S(1)}, f32[16,3072]{1,0:T(8,128)S(1)}, u32[]{:S(2)}, u32[]{:S(2)}) collective-permute-start(f32[16,3072]{1,0:T(8,128)S(1)} %fusion), channel_id=1, source_target_pairs={{0,32},{4,36},{8,40},{12,44},{16,48},{20,52},{24,56},{28,60},{32,6... | collective-permute-start | bytes 589832
  866.3 16.9 %collective-permute-start.6 = (f32[16,3072]{1,0:T(8,128)S(1)}, f32[16,3072]{1,0:T(8,128)S(1)}, u32[]{:S(2)}, u32[]{:S(2)}) collective-permute-start(f32[16,3072]{1,0:T(8,128)S(1)} %fusion), channel_id=1, source_target_pairs={{0,28},{4,32},{8,36},{12,40},{16,44},{20,48},{24,52},{28,56},{32,6... | collective-permute-start | bytes 589832
  883.2 1.3 collective-permute-start.5
  884.5 7.6 collective-permute-start.4
  892.1 5.4 collective-permute-start.3
  897.5 2.6 collective-permute-start.2
  900.1 6.3 collective-permute-start.1
  906.4 3.0 collective-permute-start
  911.3 41.9 %concatenate.4 = f32[268,3072]{1,0:T(8,128)} concatenate(f32[12,3072]{1,0:T(8,128)S(1)} %collective-permute-done.15, f32[16,3072]{1,0:T(8,128)S(1)} %collective-permute-done.14, f32[16,3072]{1,0:T(8,128)S(1)} %collective-permute-done.13, f32[16,3072]{1,0:T(8,128)S(1)} %collective-permute-done.12, f32[16,3072]{1,0:T(8,128)S(1)} %collective-permute-done.11, ...), dimensions={0} | concatenate | bytes 6586368
  953.1 1.7 constant_dynamic-slice_fusion
  955.2 1.9 copy.81
  957.2 58.0 %all-reduce.5.cloned.1.call-done = f32[12,3072]{1,0:T(8,128)} async-done(((f32[12,3072]{1,0:T(8,128)}), f32[12,3072]{1,0:T(8,128)}) %all-reduce.5.cloned.1.call-update) | async-done | bytes 147472 | tf_op jit(solution)/shard_map/psum | solution.py:82
  1015.1 1.6 slice.23
  1016.7 1.4 slice.24
  1018.1 77.2 %all-reduce.2 = (f32[768]{0:T(1024)}, f32[768]{0:T(1024)}, f32[768]{0:T(1024)}) all-reduce(f32[768]{0:T(1024)S(1)} %get-tuple-element.32, f32[768]{0:T(1024)S(1)} %get-tuple-element.35, f32[768]{0:T(1024)S(1)} %reduce_sum.89), channel_id=1, replica_groups=mesh['seq'=64,'dp'=4] {'seq','dp'}, use_global_device_ids=true, to_apply=%region_8.0 | all-reduce | flops 2304 | bytes 18432 | tf_op jit(solution)/shard_map/psum | solution.py:83
  1095.3 0.9 copy.82
  (73 shorter events, 5.0 us)
Async XLA Ops:
  7.2 165.1 %all-gather.9.cloned.1.call-start = ((), (), s32[]{:S(2)}) async-start(), calls=%async_computation.5 | async-start | bytes 9584640 | tf_op jit(solution)/shard_map/all_gather | solution.py:16
  7.9 286.3 %all-gather.11.cloned.1.call-start = ((), (), s32[]{:S(2)}) async-start(), calls=%async_computation.6 | async-start | bytes 3194880 | tf_op jit(solution)/shard_map/all_gather | solution.py:17
  8.6 409.4 %all-gather.13.cloned.1.call-start = ((), (), s32[]{:S(2)}) async-start(), calls=%async_computation.7 | async-start | bytes 3194880 | tf_op jit(solution)/shard_map/all_gather | solution.py:17
  10.4 36.4 %copy-start.9 = (f32[768]{0:T(1024)S(1)}, f32[768]{0:T(1024)}, u32[]{:S(2)}) copy-start(f32[768]{0:T(1024)} %param.9) | copy-start | bytes 9220
  10.4 36.3 %copy-start.14 = (f32[768]{0:T(1024)S(1)}, f32[768]{0:T(1024)}, u32[]{:S(2)}) copy-start(f32[768]{0:T(1024)} %param.10) | copy-start | bytes 9220
  46.2 0.6 copy-start.12
  200.1 2.3 copy-start
  202.1 1.0 copy-start.3
  202.1 1.0 copy-start.7
  203.1 0.6 copy-start.10
  208.9 1.3 copy-start.6
  211.6 91.2 %all-to-all-start.2 = ((f32[1,1,192,768]{3,1,0,2:T(1,128)}), f32[1,1,192,768]{3,1,0,2:T(1,128)S(1)}, u32[]{:S(2)}, u32[]{:S(2)}) async-start(f32[1,1,192,768]{3,1,0,2:T(1,128)} %copy.70), calls=%async_computation.2 | async-start | bytes 1179648 | tf_op jit(solution)/shard_map/all_to_all | solution.py:30
  219.3 78.7 %copy-start.2 = (f32[192,768]{1,0:T(8,128)S(1)}, f32[192,768]{1,0:T(8,128)}, u32[]{:S(2)}) copy-start(f32[192,768]{1,0:T(8,128)} %reshape.203) | copy-start | bytes 1769476
  219.3 78.7 %copy-start.15 = (f32[768]{0:T(1024)S(1)}, f32[768]{0:T(1024)}, u32[]{:S(2)}) copy-start(f32[768]{0:T(1024)} %param.13) | copy-start | bytes 9220
  219.3 569.3 %all-gather.15.cloned.1.call-start = ((), (), s32[]{:S(2)}) async-start(), calls=%async_computation.8 | async-start | bytes 9584640 | tf_op jit(solution)/shard_map/all_gather | solution.py:16
  302.8 506.3 %all-to-all-start.1 = ((f32[1,64,3,768]{3,0,2,1:T(1,128)}), f32[1,64,3,768]{3,0,2,1:T(1,128)}, u32[]{:S(2)}, u32[]{:S(2)}) async-start(f32[1,64,3,768]{3,0,2,1:T(1,128)} %reshape.219), calls=%async_computation.1 | async-start | bytes 1179648 | tf_op jit(solution)/shard_map/all_to_all | solution.py:74
  428.6 1.5 copy-start.8
  428.6 1.5 copy-start.11
  430.1 3.6 copy-start.1
  430.1 3.6 copy-start.4
  436.1 2.4 copy-start.5
  786.8 52.6 %collective-permute-start.15 = (f32[12,3072]{1,0:T(8,128)S(1)}, f32[12,3072]{1,0:T(8,128)S(1)}, u32[]{:S(2)}, u32[]{:S(2)}) collective-permute-start(f32[12,3072]{1,0:T(8,128)S(1)} %slice.25), channel_id=1, source_target_pairs={{0,64},{4,68},{8,72},{12,76},{16,80},{20,84},{24,88},{28,92},{32,9... | collective-permute-start | bytes 442376
  797.3 10.1 copy-start.13
  807.7 101.7 %copy-start.16 = (u32[256]{0:T(256)S(1)}, u32[256]{0:T(256)}, u32[]{:S(2)}) copy-start(u32[256]{0:T(256)} %constant.21) | copy-start | bytes 3076
  809.1 286.2 %all-to-all-start.3 = ((f32[1,64,3,768]{3,0,2,1:T(1,128)}), f32[1,64,3,768]{3,0,2,1:T(1,128)S(1)}, u32[]{:S(2)}, u32[]{:S(2)}) async-start(f32[1,64,3,768]{3,0,2,1:T(1,128)} %reshape.220), calls=%async_computation.3 | async-start | bytes 1179648 | tf_op jit(solution)/shard_map/all_to_all | solution.py:75
  818.8 196.3 %all-reduce.5.cloned.1.call-start = ((), (), s32[]{:S(2)}) async-start(), calls=%async_computation.4 | async-start | bytes 393216 | tf_op jit(solution)/shard_map/psum | solution.py:82
  818.8 23.1 %collective-permute-start.14 = (f32[16,3072]{1,0:T(8,128)S(1)}, f32[16,3072]{1,0:T(8,128)S(1)}, u32[]{:S(2)}, u32[]{:S(2)}) collective-permute-start(f32[16,3072]{1,0:T(8,128)S(1)} %fusion), channel_id=1, source_target_pairs={{0,60},{4,64},{8,68},{12,72},{16,76},{20,80},{24,84},{28,88},{32,9... | collective-permute-start | bytes 589832
  826.3 21.0 %collective-permute-start.13 = (f32[16,3072]{1,0:T(8,128)S(1)}, f32[16,3072]{1,0:T(8,128)S(1)}, u32[]{:S(2)}, u32[]{:S(2)}) collective-permute-start(f32[16,3072]{1,0:T(8,128)S(1)} %fusion), channel_id=1, source_target_pairs={{0,56},{4,60},{8,64},{12,68},{16,72},{20,76},{24,80},{28,84},{32,8... | collective-permute-start | bytes 589832
  830.6 17.9 %collective-permute-start.12 = (f32[16,3072]{1,0:T(8,128)S(1)}, f32[16,3072]{1,0:T(8,128)S(1)}, u32[]{:S(2)}, u32[]{:S(2)}) collective-permute-start(f32[16,3072]{1,0:T(8,128)S(1)} %fusion), channel_id=1, source_target_pairs={{0,52},{4,56},{8,60},{12,64},{16,68},{20,72},{24,76},{28,80},{32,8... | collective-permute-start | bytes 589832
  835.0 31.2 %collective-permute-start.11 = (f32[16,3072]{1,0:T(8,128)S(1)}, f32[16,3072]{1,0:T(8,128)S(1)}, u32[]{:S(2)}, u32[]{:S(2)}) collective-permute-start(f32[16,3072]{1,0:T(8,128)S(1)} %fusion), channel_id=1, source_target_pairs={{0,48},{4,52},{8,56},{12,60},{16,64},{20,68},{24,72},{28,76},{32,8... | collective-permute-start | bytes 589832
  839.4 43.7 %collective-permute-start.10 = (f32[16,3072]{1,0:T(8,128)S(1)}, f32[16,3072]{1,0:T(8,128)S(1)}, u32[]{:S(2)}, u32[]{:S(2)}) collective-permute-start(f32[16,3072]{1,0:T(8,128)S(1)} %fusion), channel_id=1, source_target_pairs={{0,44},{4,48},{8,52},{12,56},{16,60},{20,64},{24,68},{28,72},{32,7... | collective-permute-start | bytes 589832
  841.9 42.5 %collective-permute-start.9 = (f32[16,3072]{1,0:T(8,128)S(1)}, f32[16,3072]{1,0:T(8,128)S(1)}, u32[]{:S(2)}, u32[]{:S(2)}) collective-permute-start(f32[16,3072]{1,0:T(8,128)S(1)} %fusion), channel_id=1, source_target_pairs={{0,40},{4,44},{8,48},{12,52},{16,56},{20,60},{24,64},{28,68},{32,7... | collective-permute-start | bytes 589832
  847.2 44.9 %collective-permute-start.8 = (f32[16,3072]{1,0:T(8,128)S(1)}, f32[16,3072]{1,0:T(8,128)S(1)}, u32[]{:S(2)}, u32[]{:S(2)}) collective-permute-start(f32[16,3072]{1,0:T(8,128)S(1)} %fusion), channel_id=1, source_target_pairs={{0,36},{4,40},{8,44},{12,48},{16,52},{20,56},{24,60},{28,64},{32,6... | collective-permute-start | bytes 589832
  848.6 48.9 %collective-permute-start.7 = (f32[16,3072]{1,0:T(8,128)S(1)}, f32[16,3072]{1,0:T(8,128)S(1)}, u32[]{:S(2)}, u32[]{:S(2)}) collective-permute-start(f32[16,3072]{1,0:T(8,128)S(1)} %fusion), channel_id=1, source_target_pairs={{0,32},{4,36},{8,40},{12,44},{16,48},{20,52},{24,56},{28,60},{32,6... | collective-permute-start | bytes 589832
  866.3 33.9 %collective-permute-start.6 = (f32[16,3072]{1,0:T(8,128)S(1)}, f32[16,3072]{1,0:T(8,128)S(1)}, u32[]{:S(2)}, u32[]{:S(2)}) collective-permute-start(f32[16,3072]{1,0:T(8,128)S(1)} %fusion), channel_id=1, source_target_pairs={{0,28},{4,32},{8,36},{12,40},{16,44},{20,48},{24,52},{28,56},{32,6... | collective-permute-start | bytes 589832
  883.2 23.2 %collective-permute-start.5 = (f32[16,3072]{1,0:T(8,128)S(1)}, f32[16,3072]{1,0:T(8,128)S(1)}, u32[]{:S(2)}, u32[]{:S(2)}) collective-permute-start(f32[16,3072]{1,0:T(8,128)S(1)} %fusion), channel_id=1, source_target_pairs={{0,24},{4,28},{8,32},{12,36},{16,40},{20,44},{24,48},{28,52},{32,5... | collective-permute-start | bytes 589832
  884.5 26.1 %collective-permute-start.4 = (f32[16,3072]{1,0:T(8,128)S(1)}, f32[16,3072]{1,0:T(8,128)}, u32[]{:S(2)}, u32[]{:S(2)}) collective-permute-start(f32[16,3072]{1,0:T(8,128)S(1)} %fusion), channel_id=1, source_target_pairs={{0,20},{4,24},{8,28},{12,32},{16,36},{20,40},{24,44},{28,48},{32,5... | collective-permute-start | bytes 589832
  892.1 18.5 %collective-permute-start.3 = (f32[16,3072]{1,0:T(8,128)S(1)}, f32[16,3072]{1,0:T(8,128)}, u32[]{:S(2)}, u32[]{:S(2)}) collective-permute-start(f32[16,3072]{1,0:T(8,128)S(1)} %fusion), channel_id=1, source_target_pairs={{0,16},{4,20},{8,24},{12,28},{16,32},{20,36},{24,40},{28,44},{32,4... | collective-permute-start | bytes 589832
  897.5 13.1 %collective-permute-start.2 = (f32[16,3072]{1,0:T(8,128)S(1)}, f32[16,3072]{1,0:T(8,128)}, u32[]{:S(2)}, u32[]{:S(2)}) collective-permute-start(f32[16,3072]{1,0:T(8,128)S(1)} %fusion), channel_id=1, source_target_pairs={{0,12},{4,16},{8,20},{12,24},{16,28},{20,32},{24,36},{28,40},{32,4... | collective-permute-start | bytes 589832
  900.1 10.5 collective-permute-start.1
  906.4 4.9 collective-permute-start
Sparse Core Ops, SparseCore 0:
  11.7 160.5 all-gather.8
  175.8 118.3 all-gather.10
  297.7 120.3 all-gather.12
  421.6 231.4 all-gather.14
  954.9 60.1 all-reduce.4
where the time goes:
time: 1110 us; the launch traced here: 1100 us
  blocking collectives  429 us (39%)
  waiting for transfers between devices  363 us (33%)
  starting transfers between devices  118 us (11%)
  local copies, waits for them, and re-layouts  107 us (10%)
  matrix products  56.7 us (5%)
  between operations  15.1 us (1%)
  other arithmetic  13.2 us (1%)
    unnamed x1, blocking collectives  317 us
    all_gather x2, waiting for transfers between devices, fetch(): lax.all_gather(proj_part, 'seq', axis=0, tiled=True)  178 us
    all_gather x2, waiting for transfers between devices, fetch(): lax.all_gather(qkv_part, 'seq', axis=0, tiled=True)  125 us
    unnamed x16, starting transfers between devices  92.1 us
    unnamed x46, local copies, waits for them, and re-layouts  77.3 us
    psum x1, blocking collectives, on_device(): small = lax.psum((gain_product, bias_term, proj_term), ('seq', 'dp'))  77.2 us
    psum x1, waiting for transfers between devices, on_device(): share = lax.psum(share, 'dp')  58 us
    all_to_all x1, blocking collectives, on_device(): lax.all_to_all(frames, 'seq', split_axis=2, concat_axis=1, tiled=True)  34.5 us
  transfers between devices with their start and end apart: 24, of which 5 were waited for; matrix products, arithmetic and copies ran while one was open for 45% of the time, Pallas kernels for 0%

commit v1 on v0

v1 whole, which is shorter than its diff:
```python
import functools
import math

import jax
import jax.numpy as jnp
from jax import lax
from jax.experimental import pallas as pl
from jax.experimental.pallas import tpu as pltpu
from jax.sharding import PartitionSpec as P

EPSILON = 1e-06
MESH = pl.DeviceIdType.MESH
F32 = jnp.float32
BF16 = jnp.bfloat16
WIDTH = 768
HALF = 384
LANES = 128


def position():
    s = lax.axis_index("seq")
    d = lax.axis_index("dp")
    return s, d, lax.div(s, 8), lax.rem(lax.div(s, 2), 4), lax.rem(s, 2), lax.div(d, 2), lax.rem(d, 2)


def device(s, d):
    return {"seq": s, "dp": d}


def greet(s, d, z, y, xh, xl, c):
    barrier = pltpu.get_barrier_semaphore()

    def one(k, carry):
        pl.semaphore_signal(barrier, inc=1, device_id=device(lax.rem(s + k, 64), d), device_id_type=MESH)
        return carry

    lax.fori_loop(1, 64, one, 0)
    mirror, side, mate = others(s, d, xh, xl, c)
    for where in (mirror, side, mate):
        pl.semaphore_signal(barrier, inc=1, device_id=where, device_id_type=MESH)
    pl.semaphore_wait(barrier, 66)


def others(s, d, xh, xl, c):
    mirror = device(s + 1 - 2 * xh, (1 - xl) * 2 + c)
    side = device(s, (1 - xl) * 2 + c)
    mate = device(s, xl * 2 + 1 - c)
    return mirror, side, mate


def send(src, dst, send_sem, recv_sem, where):
    copy = pltpu.make_async_remote_copy(
        src_ref=src, dst_ref=dst, send_sem=send_sem, recv_sem=recv_sem, device_id=where, device_id_type=MESH
    )
    copy.start()


def wait_for(ref, sem):
    pltpu.make_async_copy(ref, ref, sem).wait()


def bring_kernel(x_ref, dy_ref, wq_ref, wp_ref, xo, dyo, wqo, wpo, loc, ss, rx, rz, ry, rm, rs, rc):
    s, d, z, y, xh, xl, c = position()
    mirror, side, mate = others(s, d, xh, xl, c)
    greet(s, d, z, y, xh, xl, c)
    holds = lax.div(z, 4) == c
    zlow = lax.rem(z, 4)

    own_q = pltpu.make_async_copy(wq_ref, wqo.at[z, y, xh], rz.at[0])
    own_q.start()

    @pl.when(holds)
    def _():
        pltpu.make_async_copy(wp_ref, wpo.at[zlow, y, xh], rz.at[1]).start()

    def z_send(k, carry):
        there = device((lax.rem(z + k, 8) * 4 + y) * 2 + xh, d)
        send(wq_ref, wqo.at[z, y, xh], ss.at[0], rz.at[0], there)

        @pl.when(holds)
        def _():
            send(wp_ref, wpo.at[zlow, y, xh], ss.at[1], rz.at[1], there)

        return carry

    lax.fori_loop(1, 8, z_send, 0)

    pltpu.make_async_copy(x_ref.at[s], xo.at[c, s], rx.at[0]).start()
    pltpu.make_async_copy(dy_ref.at[s], dyo.at[c, s], rx.at[1]).start()

    def x_send(k, carry):
        t = lax.rem(s + k, 64)
        send(x_ref.at[t], xo.at[c, s], ss.at[2], rx.at[0], device(t, d))
        return carry

    lax.fori_loop(1, 64, x_send, 0)

    def dy_send(k, carry):
        t = lax.rem(s + k, 64)
        send(dy_ref.at[t], dyo.at[c, s], ss.at[3], rx.at[1], device(t, d))
        return carry

    lax.fori_loop(1, 64, dy_send, 0)

    wait_for(wqo.at[:, y, xh], rz.at[0])
    wait_for(wpo.at[:, y, xh], rz.at[1])

    for k in range(1, 4):
        there = device((z * 4 + lax.rem(y + k, 4)) * 2 + xh, d)
        send(wqo.at[:, y, xh], wqo.at[:, y, xh], ss.at[4], ry.at[0, k], there)
        send(wpo.at[:, y, xh], wpo.at[:, y, xh], ss.at[5], ry.at[1, k], there)

    give_q = pl.ds(4 * (1 - xl), 4)
    give_p = pl.ds(2 * (1 - xl), 2)
    take_q = pl.ds(4 * xl, 4)
    take_p = pl.ds(2 * xl, 2)

    def source(k):
        return lax.rem(y + 4 - k, 4)

    for k in range(4):
        at = source(k)
        if k > 0:
            wait_for(wqo.at[:, at, xh], ry.at[0, k])
            wait_for(wpo.at[:, at, xh], ry.at[1, k])
        send(wqo.at[give_q, at, xh], wqo.at[give_q, at, xh], ss.at[6], rm.at[0, k], mirror)
        send(wpo.at[give_p, at, xh], wpo.at[give_p, at, xh], ss.at[7], rm.at[1, k], mirror)
    for k in range(4):
        at = source(k)
        wait_for(wqo.at[take_q, at, 1 - xh], rm.at[0, k])
        wait_for(wpo.at[take_p, at, 1 - xh], rm.at[1, k])
        send(wqo.at[take_q, at, 1 - xh], wqo.at[take_q, at, 1 - xh], ss.at[8], rs.at[0, k], side)
        send(wpo.at[take_p, at, 1 - xh], wpo.at[take_p, at, 1 - xh], ss.at[9], rs.at[1, k], side)

    wait_for(xo.at[c], rx.at[0])
    send(xo.at[c], xo.at[c], ss.at[10], rc.at[0], mate)
    wait_for(dyo.at[c], rx.at[1])
    send(dyo.at[c], dyo.at[c], ss.at[11], rc.at[1], mate)

    for k in range(4):
        at = source(k)
        wait_for(wqo.at[give_q, at, 1 - xh], rs.at[0, k])
        wait_for(wpo.at[give_p, at, 1 - xh], rs.at[1, k])
    wait_for(xo.at[1 - c], rc.at[0])
    wait_for(dyo.at[1 - c], rc.at[1])

    wait_for(wqo.at[pl.ds(0, 7), 0, 0], ss.at[0])

    @pl.when(holds)
    def _():
        def w(k, carry):
            wait_for(wp_ref, ss.at[1])
            return carry

        lax.fori_loop(0, 7, w, 0)

    wait_for(xo.at[0, pl.ds(0, 63)], ss.at[2])
    wait_for(xo.at[0, pl.ds(0, 63)], ss.at[3])
    wait_for(wqo.at[:, pl.ds(0, 3), 0], ss.at[4])
    wait_for(wpo.at[:, pl.ds(0, 3), 0], ss.at[5])
    for sem in (6, 8):
        wait_for(wqo.at[pl.ds(0, 4), :, 0], ss.at[sem])
    for sem in (7, 9):
        wait_for(wpo.at[pl.ds(0, 2), :, 0], ss.at[sem])
    wait_for(xo.at[0], ss.at[10])
    wait_for(xo.at[0], ss.at[11])


def bring(x, dy, wq, wp):
    dma = pltpu.SemaphoreType.DMA
    anywhere = pl.BlockSpec(memory_space=pl.ANY)
    return pl.pallas_call(
        bring_kernel,
        out_shape=(
            jax.ShapeDtypeStruct((2, 64, 9, 2, LANES), F32),
            jax.ShapeDtypeStruct((2, 64, 9, 2, LANES), F32),
            jax.ShapeDtypeStruct((8, 4, 2, 27, 4, LANES), F32),
            jax.ShapeDtypeStruct((4, 4, 2, 9, 8, LANES), F32),
        ),
        in_specs=[anywhere] * 4,
        out_specs=(anywhere,) * 4,
        scratch_shapes=[
            dma((2,)), dma((12,)), dma((2,)), dma((2,)), dma((2, 4)), dma((2, 4)), dma((2, 4)), dma((2,)),
        ],
        compiler_params=pltpu.CompilerParams(collective_id=0, has_side_effects=True),
    )(x, dy, wq, wp)


def split(v):
    high = v.astype(BF16)
    return high, (v - high.astype(F32)).astype(BF16)


def mm(a, b, ca, cb):
    return lax.dot_general(a, b, (((ca,), (cb,)), ((), ())), preferred_element_type=F32)


def mm3(a, b, ca, cb):
    return mm(a[0], b[0], ca, cb) + (mm(a[1], b[0], ca, cb) + mm(a[0], b[1], ca, cb))


def compute_kernel(
    x_ref, dy_ref, wq_ref, wp_ref, gain_ref, bias_ref,
    out_ref, dx_ref, gq_ref, gp_ref, small_ref,
    xhat, rstd, nh, nl, yh, yl, wh, wl, ph, plo, qkv, da, ah, al, dh, dl,
):
    cols = [slice(LANES * j, LANES * (j + 1)) for j in range(9)]
    gain = gain_ref[...]
    bias = bias_ref[...]
    for j in range(9):
        wh[:, cols[j]], wl[:, cols[j]] = split(wq_ref[pl.ds(j, WIDTH, stride=9), :])
    for j in range(6):
        ph[:, cols[j]], plo[:, cols[j]] = split(wp_ref[pl.ds(j, HALF, stride=6), :])
    dy_sum = jnp.zeros((1, WIDTH), F32)
    for g in range(6):
        base = (g // 3) * 1152 + (g % 3) * 6
        rows = slice(64 * g, 64 * (g + 1))
        x = jnp.concatenate([x_ref[pl.ds(base + j, 64, stride=18), :] for j in range(6)], axis=1)
        centred = x - jnp.mean(x, axis=1, keepdims=True)
        r = lax.rsqrt(jnp.mean(centred * centred, axis=1, keepdims=True) + EPSILON)
        hat = centred * r
        xhat[rows, :] = hat
        rstd[rows, :] = jnp.broadcast_to(r, (64, LANES))
        nh[rows, :], nl[rows, :] = split(hat * gain + bias)
        y = jnp.concatenate([dy_ref[pl.ds(base + j, 64, stride=18), :] for j in range(6)], axis=1)
        yh[rows, :], yl[rows, :] = split(y)
        dy_sum = dy_sum + jnp.sum(y, axis=0, keepdims=True)
    for t in range(3):
        part = slice(HALF * t, HALF * (t + 1))
        qkv[:, part] = mm3((nh[...], nl[...]), (wh[:, part], wl[:, part]), 1, 0)
    da[...] = mm3((yh[...], yl[...]), (ph[...], plo[...]), 1, 1)
    left = lax.broadcasted_iota(jnp.int32, (LANES, LANES), 1) < 64
    row = lax.broadcasted_iota(jnp.int32, (2 * LANES, LANES), 0)
    col = lax.broadcasted_iota(jnp.int32, (2 * LANES, LANES), 1)
    same = ((row % LANES) < 64) == (col < 64)

    def stacked(v):
        return jnp.concatenate([jnp.where(left, v, 0.0), jnp.where(left, 0.0, v)], axis=0)

    def joined(v):
        return jnp.where(left, v[:LANES], v[LANES:])

    scale = 0.125
    for i in range(3):
        rows = slice(LANES * i, LANES * (i + 1))
        for h in range(3):
            q = split(stacked(qkv[rows, cols[h]] * scale))
            k = split(qkv[rows, cols[3 + h]])
            v = split(qkv[rows, cols[6 + h]])
            a = split(stacked(da[rows, cols[h]]))
            scores = jnp.where(same, mm3(q, k, 1, 1), -1e30)
            e = jnp.exp(scores - jnp.max(scores, axis=1, keepdims=True))
            probs = e / jnp.sum(e, axis=1, keepdims=True)
            pair = split(probs)
            ah[rows, cols[h]], al[rows, cols[h]] = split(joined(mm3(pair, v, 1, 0)))
            dh[rows, cols[6 + h]], dl[rows, cols[6 + h]] = split(mm3(pair, a, 0, 0))
            t = mm3(a, v, 1, 1) * probs
            ds = split(t - probs * jnp.sum(t, axis=1, keepdims=True))
            dh[rows, cols[h]], dl[rows, cols[h]] = split(joined(mm3(ds, k, 1, 0)) * scale)
            dh[rows, cols[3 + h]], dl[rows, cols[3 + h]] = split(mm3(ds, q, 0, 0))
    for t in range(2):
        part = slice(HALF * t, HALF * (t + 1))
        o = mm3((ah[...], al[...]), (ph[:, part], plo[:, part]), 1, 0)
        for g in range(6):
            for j in range(3):
                out_ref[pl.ds((g // 3) * 1152 + (g % 3) * 6 + 3 * t + j, 64, stride=18), :] = (
                    o[64 * g : 64 * (g + 1), cols[j]]
                )
        w = mm3((ah[...], al[...]), (yh[:, part], yl[:, part]), 0, 0)
        for j in range(3):
            gp_ref[pl.ds(3 * t + j, HALF, stride=6), :] = w[:, cols[j]]
    for t in range(3):
        part = slice(HALF * t, HALF * (t + 1))
        w = mm3((nh[...], nl[...]), (dh[:, part], dl[:, part]), 0, 0)
        for j in range(3):
            gq_ref[pl.ds(3 * t + j, WIDTH, stride=9), :] = w[:, cols[j]]
    gain_sum = jnp.zeros((1, WIDTH), F32)
    bias_sum = jnp.zeros((1, WIDTH), F32)
    for i in range(3):
        dn = mm3((dh[128 * i : 128 * (i + 1), :], dl[128 * i : 128 * (i + 1), :]), (wh[...], wl[...]), 1, 1)
        for half in range(2):
            g = 2 * i + half
            rows = slice(64 * g, 64 * (g + 1))
            n = dn[64 * half : 64 * (half + 1)]
            hat = xhat[rows, :]
            gain_sum = gain_sum + jnp.sum(n * hat, axis=0, keepdims=True)
            bias_sum = bias_sum + jnp.sum(n, axis=0, keepdims=True)
            n = n * gain
            m1 = jnp.mean(n, axis=1, keepdims=True)
            m2 = jnp.mean(n * hat, axis=1, keepdims=True)
            r = rstd[rows, 0:1]
            dx = r * (n - m1 - hat * m2)
            for j in range(6):
                dx_ref[pl.ds((g // 3) * 1152 + (g % 3) * 6 + j, 64, stride=18), :] = dx[:, cols[j]]
    for n, v in enumerate((gain_sum, bias_sum, dy_sum * 0.5)):
        for j in range(6):
            small_ref[6 * n + j : 6 * n + j + 1, :] = v[:, cols[j]]
    small_ref[18:24, :] = jnp.zeros((6, LANES), F32)


def compute(x, dy, wq, wp, gain, bias):
    vmem = pl.BlockSpec(memory_space=pltpu.VMEM)
    tokens = HALF
    return pl.pallas_call(
        compute_kernel,
        out_shape=(
            jax.ShapeDtypeStruct((2304, LANES), F32),
            jax.ShapeDtypeStruct((2304, LANES), F32),
            jax.ShapeDtypeStruct((6912, LANES), F32),
            jax.ShapeDtypeStruct((2304, LANES), F32),
            jax.ShapeDtypeStruct((24, LANES), F32),
        ),
        in_specs=[vmem] * 6,
        out_specs=(vmem,) * 5,
        scratch_shapes=[
            pltpu.VMEM((tokens, WIDTH), F32),
            pltpu.VMEM((tokens, LANES), F32),
            pltpu.VMEM((tokens, WIDTH), BF16),
            pltpu.VMEM((tokens, WIDTH), BF16),
            pltpu.VMEM((tokens, WIDTH), BF16),
            pltpu.VMEM((tokens, WIDTH), BF16),
            pltpu.VMEM((WIDTH, 3 * HALF), BF16),
            pltpu.VMEM((WIDTH, 3 * HALF), BF16),
            pltpu.VMEM((HALF, WIDTH), BF16),
            pltpu.VMEM((HALF, WIDTH), BF16),
            pltpu.VMEM((tokens, 3 * HALF), F32),
            pltpu.VMEM((tokens, HALF), F32),
            pltpu.VMEM((tokens, HALF), BF16),
            pltpu.VMEM((tokens, HALF), BF16),
            pltpu.VMEM((tokens, 3 * HALF), BF16),
            pltpu.VMEM((tokens, 3 * HALF), BF16),
        ],
        compiler_params=pltpu.CompilerParams(vmem_limit_bytes=50 * 1024 * 1024),
    )(x, dy, wq, wp, gain, bias)


def give_kernel(
    o_ref, dx_ref, gq_ref, gp_ref, sm_ref, of, df, rq, rp, so,
    ob, db, q1, p1, q2, p2, qa, pa, qy, py, qz, pz, qf, pf, qs, ps, pt, smx, smy, smz, sms, smc,
    ss, rb, r1, r2, ry, rz, rs, rc, ro, sa, ra,
):
    s, d, z, y, xh, xl, c = position()
    mirror, side, mate = others(s, d, xh, xl, c)
    greet(s, d, z, y, xh, xl, c)
    holds = lax.div(z, 4) == c
    mine_q, mine_p = 4 * xl, 2 * xl
    yours_q, yours_p = 4 * (1 - xl), 2 * (1 - xl)
    oxh = 1 - xh

    def ydst(k):
        return lax.rem(y + k, 4)

    order = (1, 2, 3, 0)
    for k in order:
        at = ydst(k)
        send(gq_ref.at[pl.ds(yours_q, 4), at, oxh], q1.at[k], ss.at[0], r1.at[0, k], side)
        send(gp_ref.at[pl.ds(yours_p, 2), at, oxh], p1.at[k], ss.at[1], r1.at[1, k], side)
    send(o_ref.at[1 - c], ob, ss.at[2], rb.at[0], mate)
    send(dx_ref.at[1 - c], db, ss.at[3], rb.at[1], mate)
    smx[0] = sm_ref[...]
    send(smx.at[0], smx.at[1], ss.at[4], ra.at[0], mirror)

    def back(own, buf, out, k_recv, k_send, k_out):
        wait_for(buf, rb.at[k_recv])

        def add(i, carry):
            buf[i] = buf[i] + own[c, i]
            return carry

        lax.fori_loop(0, 64, add, 0)
        pltpu.make_async_copy(buf.at[s], out.at[s], ro.at[k_out]).start()

        def one(k, carry):
            t = lax.rem(s + k, 64)
            send(buf.at[t], out.at[s], ss.at[k_send], ro.at[k_out], device(t, d))
            return carry

        lax.fori_loop(1, 64, one, 0)

    for k in order:
        at = ydst(k)
        wait_for(q1.at[k], r1.at[0, k])
        wait_for(p1.at[k], r1.at[1, k])

        for i in range(4):
            q1[k, i] = q1[k, i] + gq_ref[mine_q + i, at, oxh]
        for i in range(2):
            p1[k, i] = p1[k, i] + gp_ref[mine_p + i, at, oxh]
        send(q1.at[k], q2.at[k], ss.at[5], r2.at[0, k], mirror)
        send(p1.at[k], p2.at[k], ss.at[6], r2.at[1, k], mirror)
        if k == 1:
            back(o_ref, ob, of, 0, 7, 0)
        if k == 2:
            back(dx_ref, db, df, 1, 8, 1)

    wait_for(smx.at[1], ra.at[0])
    smy[y] = smx[0] + smx[1]
    for k in range(1, 4):
        there = device((z * 4 + ydst(k)) * 2 + xh, d)
        send(smy.at[y], smy.at[y], ss.at[9], ra.at[1], there)

    for k in order:
        at = ydst(k)
        wait_for(q2.at[k], r2.at[0, k])
        wait_for(p2.at[k], r2.at[1, k])
        for i in range(4):
            qa[k, yours_q + i] = q2[k, i] + gq_ref[yours_q + i, at, xh]
            qa[k, mine_q + i] = gq_ref[mine_q + i, at, xh]
        for i in range(2):
            pa[k, yours_p + i] = p2[k, i] + gp_ref[yours_p + i, at, xh]
            pa[k, mine_p + i] = gp_ref[mine_p + i, at, xh]
        if k > 0:
            there = device((z * 4 + at) * 2 + xh, d)
            send(qa.at[k], qy.at[k], ss.at[10], ry.at[0, k], there)
            send(pa.at[k], py.at[k], ss.at[11], ry.at[1, k], there)

    wait_for(smy.at[pl.ds(0, 3)], ra.at[1])
    smz[z] = (smy[0] + smy[1]) + (smy[2] + smy[3])

    def sz(k, carry):
        there = device((lax.rem(z + k, 8) * 4 + y) * 2 + xh, d)
        send(smz.at[z], smz.at[z], ss.at[12], ra.at[2], there)
        return carry

    lax.fori_loop(1, 8, sz, 0)

    for k in range(1, 4):
        wait_for(qy.at[k], ry.at[0, k])
        wait_for(py.at[k], ry.at[1, k])

    def zq(i, carry):
        qa[0, i] = (qa[0, i] + qy[1, i]) + (qy[2, i] + qy[3, i])
        return carry

    lax.fori_loop(0, 8, zq, 0)

    def zp(i, carry):
        pa[0, i] = (pa[0, i] + py[1, i]) + (py[2, i] + py[3, i])
        return carry

    lax.fori_loop(0, 4, zp, 0)

    def zs(k, carry):
        at = lax.rem(z + k, 8)
        there = device((at * 4 + y) * 2 + xh, d)
        send(qa.at[0, at], qz.at[z], ss.at[13], rz.at[0], there)

        @pl.when(lax.div(at, 4) == c)
        def _():
            send(pa.at[0, lax.rem(at, 4)], pz.at[z], ss.at[14], rz.at[1], there)

        return carry

    lax.fori_loop(1, 8, zs, 0)
    qz[z] = qa[0, z]

    @pl.when(holds)
    def _():
        pz[z] = pa[0, lax.rem(z, 4)]

    wait_for(smz.at[pl.ds(0, 7)], ra.at[2])
    total = ((smz[0] + smz[1]) + (smz[2] + smz[3])) + ((smz[4] + smz[5]) + (smz[6] + smz[7]))
    sms[0] = total
    send(sms.at[0], sms.at[1], ss.at[15], ra.at[3], side)

    wait_for(qz.at[pl.ds(0, 7)], rz.at[0])
    qf[...] = ((qz[0] + qz[1]) + (qz[2] + qz[3])) + ((qz[4] + qz[5]) + (qz[6] + qz[7]))
    send(qf, qs, ss.at[16], rs.at[0], side)

    @pl.when(holds)
    def _():
        wait_for(pz.at[pl.ds(0, 7)], rz.at[1])
        pf[...] = ((pz[0] + pz[1]) + (pz[2] + pz[3])) + ((pz[4] + pz[5]) + (pz[6] + pz[7]))
        send(pf, ps, ss.at[17], rs.at[1], side)

    wait_for(sms.at[1], ra.at[3])
    smc[0] = sms[0] + sms[1]
    send(smc.at[0], smc.at[1], ss.at[18], ra.at[4], mate)
    wait_for(qs, rs.at[0])
    wait_for(qf, ss.at[16])
    qf[...] = qf[...] + qs[...]
    keep = pltpu.make_async_copy(qf, rq.at[c], sa.at[0])
    keep.start()
    send(qf, rq.at[c], ss.at[19], rc.at[0], mate)

    @pl.when(holds)
    def _():
        wait_for(ps, rs.at[1])
        pt[...] = pf[...] + ps[...]
        pltpu.make_async_copy(pt, rp, sa.at[1]).start()
        send(pt, rp, ss.at[20], rc.at[1], mate)

    wait_for(smc.at[1], ra.at[4])
    so[...] = smc[0] + smc[1]
    wait_for(qf, rc.at[0])
    keep.wait()

    @pl.when(holds)
    def _():
        wait_for(pt, sa.at[1])
        wait_for(pt, ss.at[20])
        wait_for(pf, ss.at[17])
        wait_for(pz.at[pl.ds(0, 3)], ss.at[14])

    @pl.when(jnp.logical_not(holds))
    def _():
        wait_for(pt, rc.at[1])
        wait_for(pz.at[pl.ds(0, 4)], ss.at[14])

    wait_for(ob, ro.at[0])
    wait_for(db, ro.at[1])
    wait_for(q1, ss.at[0])
    wait_for(p1, ss.at[1])
    wait_for(ob, ss.at[2])
    wait_for(db, ss.at[3])
    wait_for(smx.at[0], ss.at[4])
    wait_for(q2, ss.at[5])
    wait_for(p2, ss.at[6])
    wait_for(ob.at[pl.ds(0, 63)], ss.at[7])
    wait_for(db.at[pl.ds(0, 63)], ss.at[8])
    wait_for(smy.at[pl.ds(0, 3)], ss.at[9])
    wait_for(qa.at[pl.ds(1, 3)], ss.at[10])
    wait_for(pa.at[pl.ds(1, 3)], ss.at[11])
    wait_for(smz.at[pl.ds(0, 7)], ss.at[12])
    wait_for(qz.at[pl.ds(0, 7)], ss.at[13])
    wait_for(sms.at[0], ss.at[15])
    wait_for(smc.at[0], ss.at[18])
    wait_for(qf, ss.at[19])


def give(o, dx, gq, gp, sm):
    dma = pltpu.SemaphoreType.DMA
    anywhere = pl.BlockSpec(memory_space=pl.ANY)
    vmem = pl.BlockSpec(memory_space=pltpu.VMEM)
    act = (64, 9, 2, LANES)
    q, p, sml = (27, 4, LANES), (9, 8, LANES), (24, LANES)

    def buf(*shape):
        return pltpu.VMEM(shape, F32)

    return pl.pallas_call(
        give_kernel,
        out_shape=(
            jax.ShapeDtypeStruct(act, F32),
            jax.ShapeDtypeStruct(act, F32),
            jax.ShapeDtypeStruct((2,) + q, F32),
            jax.ShapeDtypeStruct(p, F32),
            jax.ShapeDtypeStruct(sml, F32),
        ),
        in_specs=[vmem] * 5,
        out_specs=(anywhere, anywhere, anywhere, anywhere, vmem),
        scratch_shapes=[
            buf(*act), buf(*act),
            buf(4, 4, *q), buf(4, 2, *p), buf(4, 4, *q), buf(4, 2, *p),
            buf(4, 8, *q), buf(4, 4, *p), buf(4, 8, *q), buf(4, 4, *p),
            buf(8, *q), buf(8, *p), buf(*q), buf(*p), buf(*q), buf(*p), buf(*p),
            buf(2, *sml), buf(4, *sml), buf(8, *sml), buf(2, *sml), buf(2, *sml),
            dma((21,)), dma((2,)), dma((2, 4)), dma((2, 4)), dma((2, 4)), dma((2,)), dma((2,)), dma((2,)),
            dma((2,)), dma((2,)), dma((5,)),
        ],
        compiler_params=pltpu.CompilerParams(
            collective_id=1, has_side_effects=True, vmem_limit_bytes=50 * 1024 * 1024
        ),
    )(o, dx, gq, gp, sm)


def on_device(
    frames, out_cotangent, layer_norm_gain, layer_norm_bias, qkv_weight, proj_weight, proj_bias
):
    c = lax.rem(lax.axis_index("dp"), 2)
    blocks = (64, 9, 2, LANES)
    half = lax.dynamic_index_in_dim(qkv_weight.reshape(12, 3, 2, HALF), c, axis=2, keepdims=False)
    x, dy, wq, wp = bring(
        frames.reshape(blocks),
        out_cotangent.reshape(blocks),
        half.reshape(27, 4, LANES),
        proj_weight.reshape(9, 8, LANES),
    )
    o, dx, gq, gp, small = compute(
        x.reshape(2304, LANES),
        dy.reshape(2304, LANES),
        wq.reshape(6912, LANES),
        wp.reshape(2304, LANES),
        layer_norm_gain.reshape(1, WIDTH),
        layer_norm_bias.reshape(1, WIDTH),
    )
    of, df, rq, rp, so = give(
        o.reshape((2,) + blocks),
        dx.reshape((2,) + blocks),
        gq.reshape(8, 4, 2, 27, 4, LANES),
        gp.reshape(4, 4, 2, 9, 8, LANES),
        small,
    )
    sums = so[:18].reshape(3, WIDTH)
    grad_qkv = jnp.transpose(rq.reshape(2, 12, 3, HALF), (1, 2, 0, 3)).reshape(12, 3 * WIDTH)
    return (
        frames + of.reshape(frames.shape) + proj_bias,
        out_cotangent + df.reshape(frames.shape),
        sums[0],
        sums[1],
        grad_qkv,
        rp.reshape(12, WIDTH),
        sums[2],
    )


def solution(mesh):
    return jax.shard_map(
        on_device,
        mesh=mesh,
        in_specs=(
            P("dp", "seq", None, None),
            P("dp", "seq", None, None),
            P(),
            P(),
            P("seq", None),
            P("seq", None),
            P(),
        ),
        out_specs=(
            P("dp", "seq", None, None),
            P("dp", "seq", None, None),
            P(),
            P(),
            P("seq", None),
            P("seq", None),
            P(),
        ),
        check_vma=False,
    )
```

time: 1110 us -> 228 us (0.21)
  blocking collectives: 429 us -> 0 us
  waiting for transfers between devices: 363 us -> 0 us
  Pallas kernels: 0 us -> 213 us
  starting transfers between devices: 118 us -> 0 us
  local copies, waits for them, and re-layouts: 107 us -> 12.4 us
  matrix products: 56.7 us -> 0 us
  between operations: 15.1 us -> 0.73 us
  other arithmetic: 13.2 us -> 1.78 us
    unnamed x1 -> x0, blocking collectives: 317 us -> none
    all_gather x4 -> x0, waiting for transfers between devices: 303 us -> none  [the longest x2 178 us: fetch(): lax.all_gather(proj_part, 'seq', axis=0, tiled=True)]
    pallas_call x0 -> x3, Pallas kernels: none -> 213 us  [the longest x1 103 us: give(): pl.pallas_call(give_kernel, out_shape=(jax.ShapeDtypeStruct(act, F32), ja...]
    unnamed x16 -> x0, starting transfers between devices: 92.1 us -> none
    psum x1 -> x0, blocking collectives: 77.2 us -> none  [on_device(): small = lax.psum((gain_product, bias_term, proj_term), ('seq', 'dp'))]
    unnamed x46 -> x8, local copies, waits for them, and re-layouts: 77.3 us -> 1.6 us
    psum x1 -> x0, waiting for transfers between devices: 58 us -> none  [on_device(): share = lax.psum(share, 'dp')]
    dot_general x12 -> x0, matrix products: 56.7 us -> none  [the longest x1 11.1 us: on_device(): qkv = jnp.dot(norm_output, full_qkv, precision=highest)]
  transfers between devices with their start and end apart: 24 -> 0, of which waited for: 5 -> 0; matrix products, arithmetic and copies ran while one was open for 45% -> 0% of each run, Pallas kernels for 0% -> 0%
where the time goes in v1:
time: 228 us
  Pallas kernels  213 us (93%)
  local copies, waits for them, and re-layouts  12.4 us (5%)
    pallas_call x1, Pallas kernels, give(): pl.pallas_call(give_kernel, out_shape=(jax.ShapeDtypeStruct(act, F32), ja...  103 us
    pallas_call x1, Pallas kernels, bring(): pl.pallas_call(bring_kernel, out_shape=(jax.ShapeDtypeStruct((2, 64, 9, 2...  83.1 us
    pallas_call x1, Pallas kernels, compute(): pl.pallas_call(compute_kernel, out_shape=(jax.ShapeDtypeStruct((2304, LAN...  26.4 us

profile of v1, /device:TPU:1, one launch (start us, length us, event | category | flops | bytes accessed | tf_op | source)
XLA Modules:
  0.0 227.8 jit_solution(2969624171152428244)
XLA Ops:
  0.6 0.0 copy-start.2
  0.7 0.7 reshape.94.gain_ref
  1.4 0.7 reshape.95.bias_ref
  2.1 1.4 reshape.89.wp_ref
  3.5 1.0 reshape.87
  4.5 0.7 constant_dynamic-slice_fusion
  5.2 2.2 reshape.85.x_ref
  7.3 0.0 copy-done.2
  7.3 1.1 reshape.86.dy_ref
  8.4 83.1 %shard_map.126 = (f32[2,64,9,2,128]{4,3,2,1,0:T(2,128)}, f32[2,64,9,2,128]{4,3,2,1,0:T(2,128)}, f32[8,4,2,27,4,128]{5,4,3,2,1,0:T(4,128)}, f32[4,4,2,9,8,128]{5,4,3,2,1,0:T(8,128)}) custom-call(f32[64,9,2,128]{3,2,1,0:T(2,128)} %reshape.85.x_ref, f32[64,9,2,128]{3,2,1,0:T(2,128)} %reshape.86.dy_ref, f32[27,4,128]{2,1,0:T(4,128)} %bitcast.29, ...), custom_call_target="tpu_custom_call" | custom-call | tf_op jit(solution)/shard_map/pallas_call | solution.py:172
  91.5 26.4 %shard_map.127 = (f32[2304,128]{1,0:T(8,128)S(1)}, f32[2304,128]{1,0:T(8,128)S(1)}, f32[6912,128]{1,0:T(8,128)}, f32[2304,128]{1,0:T(8,128)S(1)}, f32[24,128]{1,0:T(8,128)S(1)}) custom-call(f32[2304,128]{1,0:T(8,128)} %bitcast.25, f32[2304,128]{1,0:T(8,128)} %bitcast.26, f32[6912,128]{1,0:T(8,128)} %bitcast.23, f32[2304,128]{1,0:T(8,128)} %bitcast.27, ...), custom_call_target="tpu_custom_call" | custom-call | tf_op jit(solution)/shard_map/pallas_call | solution.py:304
  117.9 0.0 copy-start
  117.9 1.0 copy-done
  118.9 103.4 %shard_map.128 = (f32[64,9,2,128]{3,2,1,0:T(2,128)S(1)}, f32[64,9,2,128]{3,2,1,0:T(2,128)S(1)}, f32[2,27,4,128]{3,2,1,0:T(4,128)S(1)}, f32[9,8,128]{2,1,0:T(8,128)S(1)}, f32[24,128]{1,0:T(8,128)S(1)}) custom-call(f32[2,64,9,2,128]{4,3,2,1,0:T(2,128)S(1)} %bitcast.20, f32[2,64,9,2,128]{4,3,2,1,0:T(2,128)S(1)} %bitcast.21, f32[8,4,2,27,4,128]{5,4,3,2,1,0:T(4,128)} %bitcast.24, ...), custom_call_target="tpu_custom_call" | custom-call | tf_op jit(solution)/shard_map/pallas_call | solution.py:541
  222.4 0.0 copy-start.1
  222.4 0.0 copy-start.3
  222.4 0.5 reshape.100
  222.9 0.6 copy-done.1
  223.4 0.0 copy-done.3
  223.4 0.9 add_add_fusion
  224.3 0.6 slice_bitcast_fusion
  224.9 0.6 reshape.104
  225.5 0.1 reshape.102
  225.6 0.1 copy.18
  225.7 0.8 reshape.103
  226.4 0.5 reshape.101
  226.9 0.9 add.22
Async XLA Ops:
  0.6 6.7 %copy-start.2 = (f32[1,1,192,768]{3,2,1,0:T(8,128)S(1)}, f32[1,1,192,768]{3,2,1,0:T(8,128)}, u32[]{:S(2)}) copy-start(f32[1,1,192,768]{3,2,1,0:T(8,128)} %param.8) | copy-start | bytes 1769476
  117.9 1.0 copy-start
  222.4 1.1 copy-start.1
  222.4 1.1 copy-start.3

commit v2 on v1

v2 whole, which is shorter than its diff:
```python
import functools
import math

import jax
import jax.numpy as jnp
from jax import lax
from jax.experimental import pallas as pl
from jax.experimental.pallas import tpu as pltpu
from jax.sharding import PartitionSpec as P

EPSILON = 1e-06
MESH = pl.DeviceIdType.MESH
F32 = jnp.float32
BF16 = jnp.bfloat16
WIDTH = 768
HALF = 384
LANES = 128


def position():
    s = lax.axis_index("seq")
    d = lax.axis_index("dp")
    return s, d, lax.div(s, 8), lax.rem(lax.div(s, 2), 4), lax.rem(s, 2), lax.div(d, 2), lax.rem(d, 2)


def device(s, d):
    return {"seq": s, "dp": d}


def greet(s, d, z, y, xh, xl, c, *more):
    barrier = pltpu.get_barrier_semaphore()

    def one(k, carry):
        pl.semaphore_signal(barrier, inc=1, device_id=device(lax.rem(s + k, 64), d), device_id_type=MESH)
        return carry

    lax.fori_loop(1, 64, one, 0)
    near = others(s, d, xh, xl, c) + more
    for where in near:
        pl.semaphore_signal(barrier, inc=1, device_id=where, device_id_type=MESH)
    pl.semaphore_wait(barrier, 63 + len(near))


def others(s, d, xh, xl, c):
    mirror = device(s + 1 - 2 * xh, (1 - xl) * 2 + c)
    side = device(s, (1 - xl) * 2 + c)
    mate = device(s, xl * 2 + 1 - c)
    return mirror, side, mate


def send(src, dst, send_sem, recv_sem, where):
    copy = pltpu.make_async_remote_copy(
        src_ref=src, dst_ref=dst, send_sem=send_sem, recv_sem=recv_sem, device_id=where, device_id_type=MESH
    )
    copy.start()


def wait_for(ref, sem):
    pltpu.make_async_copy(ref, ref, sem).wait()


ORDER = (0, 1, 7, 2, 6, 3, 5, 4)


def bring_kernel(x_ref, dy_ref, wq_ref, wp_ref, xo, dyo, wqo, wpo, ss, rx, rz, ry, rm, rs, rc):
    s, d, z, y, xh, xl, c = position()
    mirror, side, mate = others(s, d, xh, xl, c)
    greet(s, d, z, y, xh, xl, c)

    def zdev(k):
        return device((lax.rem(z + k + 8, 8) * 4 + y) * 2 + xh, d)

    def ydev(k):
        return device((z * 4 + lax.rem(y + k, 4)) * 2 + xh, d)

    def both(j, q_job, p_job):
        at = lax.rem(z + j, 8)
        q_job(at)

        @pl.when(lax.div(at, 4) == c)
        def _():
            p_job(lax.rem(at, 4))

    def along_z(j, to, there, src_q=None, src_p=None):
        both(
            j,
            lambda at: send(wqo.at[at, y, xh] if src_q is None else src_q, wqo.at[at, y, xh], ss.at[0], rz.at[0, to], there),
            lambda at: send(wpo.at[at, y, xh] if src_p is None else src_p, wpo.at[at, y, xh], ss.at[1], rz.at[1, to], there),
        )

    def z_stage(j):
        if j == 0:
            along_z(0, 7, zdev(1), wq_ref, wp_ref)
            along_z(0, 1, zdev(-1), wq_ref, wp_ref)
            both(
                0,
                lambda at: pltpu.make_async_copy(wq_ref, wqo.at[at, y, xh], rz.at[0, 0]).start(),
                lambda at: pltpu.make_async_copy(wp_ref, wpo.at[at, y, xh], rz.at[1, 0]).start(),
            )
        both(
            j,
            lambda at: wait_for(wqo.at[at, y, xh], rz.at[0, j]),
            lambda at: wait_for(wpo.at[at, y, xh], rz.at[1, j]),
        )
        if j in (7, 6):
            along_z(j, j - 1, zdev(1))
        if j in (1, 2):
            along_z(j, j + 1, zdev(-1))
        if j == 5:
            @pl.when(c == 0)
            def _():
                along_z(5, 4, zdev(1))
        if j == 3:
            @pl.when(c == 1)
            def _():
                along_z(3, 4, zdev(-1))

    def y_send(j):
        for k in (1, 3):
            both(
                j,
                lambda at: send(wqo.at[at, y, xh], wqo.at[at, y, xh], ss.at[4], ry.at[0, j, k], ydev(k)),
                lambda at: send(wpo.at[at, y, xh], wpo.at[at, y, xh], ss.at[5], ry.at[1, j, k], ydev(k)),
            )

    def across(j, k):
        row = lax.rem(y + 4 - k, 4)
        hq, hp = pl.ds(27 * (1 - xl), 27), pl.ds(9 * (1 - xl), 9)

        def q(at):
            ref = wqo.at[at, row, xh, hq]
            send(ref, ref, ss.at[6], rm.at[0, j, row], mirror)

        def p(at):
            ref = wpo.at[at, row, xh, hp]
            send(ref, ref, ss.at[7], rm.at[1, j, row], mirror)

        both(j, q, p)

    def y_wait(j, k):
        row = lax.rem(y + 4 - k, 4)
        both(
            j,
            lambda at: wait_for(wqo.at[at, row, xh], ry.at[0, j, k]),
            lambda at: wait_for(wpo.at[at, row, xh], ry.at[1, j, k]),
        )

    def y_pass(j, k):
        h = 0 if k == 1 else 1
        row = lax.rem(y + 4 - k, 4)

        def q(at):
            ref = wqo.at[at, row, xh, pl.ds(27 * h, 27)]
            send(ref, ref, ss.at[4], ry.at[0, j, 2], ydev(k))

        def p(at):
            ref = wpo.at[at, row, xh, pl.ds(9 * h, 9)]
            send(ref, ref, ss.at[5], ry.at[1, j, 2], ydev(k))

        both(j, q, p)

    def forward(j, k):
        row = lax.rem(y + 4 - k, 4)
        hq, hp = pl.ds(27 * xl, 27), pl.ds(9 * xl, 9)

        def q(at):
            ref = wqo.at[at, row, 1 - xh, hq]
            wait_for(ref, rm.at[0, j, row])
            send(ref, ref, ss.at[8], rs.at[0, j, row], side)

        def p(at):
            ref = wpo.at[at, row, 1 - xh, hp]
            wait_for(ref, rm.at[1, j, row])
            send(ref, ref, ss.at[9], rs.at[1, j, row], side)

        both(j, q, p)

    pltpu.make_async_copy(x_ref.at[s], xo.at[c, s], rx.at[0]).start()
    pltpu.make_async_copy(dy_ref.at[s], dyo.at[c, s], rx.at[1]).start()

    def spread(n, first, last):
        src, dst = ((x_ref, xo), (dy_ref, dyo))[n]

        def one(k, carry):
            t = lax.rem(s + k, 64)
            send(src.at[t], dst.at[c, s], ss.at[2 + n], rx.at[n], device(t, d))
            return carry

        lax.fori_loop(first, last, one, 0)

    for t in range(11):
        if t < 8:
            z_stage(ORDER[t])
            y_send(ORDER[t])
            across(ORDER[t], 0)
        if 1 <= t < 9:
            j = ORDER[t - 1]
            for k in (1, 3):
                y_wait(j, k)
                y_pass(j, k)
                across(j, k)
        if 2 <= t < 10:
            j = ORDER[t - 2]
            y_wait(j, 2)
            across(j, 2)
            forward(j, 0)
        if 3 <= t < 11:
            j = ORDER[t - 3]
            for k in (1, 3, 2):
                forward(j, k)
        if t == 1:
            spread(0, 1, 17)
        if t == 2:
            spread(0, 17, 33)
        if t == 3:
            spread(0, 33, 49)
        if t == 4:
            spread(0, 49, 64)
        if t == 5:
            spread(1, 1, 17)
        if t == 6:
            spread(1, 17, 33)
        if t == 7:
            spread(1, 33, 49)
        if t == 8:
            spread(1, 49, 64)

    wait_for(xo.at[c], rx.at[0])
    send(xo.at[c], xo.at[c], ss.at[10], rc.at[0], mate)
    wait_for(dyo.at[c], rx.at[1])
    send(dyo.at[c], dyo.at[c], ss.at[11], rc.at[1], mate)

    def last(at, carry):
        for row in range(4):
            ref = wqo.at[at, row, 1 - xh, pl.ds(27 * (1 - xl), 27)]
            wait_for(ref, rs.at[0, lax.rem(at + 8 - z, 8), row])

            @pl.when(lax.div(at, 4) == c)
            def _():
                ref = wpo.at[lax.rem(at, 4), row, 1 - xh, pl.ds(9 * (1 - xl), 9)]
                wait_for(ref, rs.at[1, lax.rem(at + 8 - z, 8), row])

        return carry

    lax.fori_loop(0, 8, last, 0)
    wait_for(xo.at[1 - c], rc.at[0])
    wait_for(dyo.at[1 - c], rc.at[1])

    wait_for(wqo.at[pl.ds(0, 7), 0, 0], ss.at[0])
    z_sends = (0, 7, 6, 0, 1, 2)
    for j in z_sends:
        @pl.when(lax.div(lax.rem(z + j, 8), 4) == c)
        def _():
            wait_for(wp_ref, ss.at[1])
    for j, core in ((5, 0), (3, 1)):
        @pl.when(jnp.logical_and(c == core, lax.div(lax.rem(z + j, 8), 4) == c))
        def _():
            wait_for(wp_ref, ss.at[1])
    wait_for(xo.at[0, pl.ds(0, 63)], ss.at[2])
    wait_for(xo.at[0, pl.ds(0, 63)], ss.at[3])
    wait_for(wqo.at[:, pl.ds(0, 3), 0], ss.at[4])
    wait_for(wpo.at[:, pl.ds(0, 3), 0], ss.at[5])
    for sem in (6, 8):
        wait_for(wqo.at[:, :, 0, pl.ds(0, 27)], ss.at[sem])
    for sem in (7, 9):
        wait_for(wpo.at[:, :, 0, pl.ds(0, 9)], ss.at[sem])
    wait_for(xo.at[0], ss.at[10])
    wait_for(xo.at[0], ss.at[11])


def bring(x, dy, wq, wp):
    dma = pltpu.SemaphoreType.DMA
    anywhere = pl.BlockSpec(memory_space=pl.ANY)
    return pl.pallas_call(
        bring_kernel,
        out_shape=(
            jax.ShapeDtypeStruct((2, 64, 9, 2, LANES), F32),
            jax.ShapeDtypeStruct((2, 64, 9, 2, LANES), F32),
            jax.ShapeDtypeStruct((8, 4, 2, 54, 2, LANES), F32),
            jax.ShapeDtypeStruct((4, 4, 2, 18, 4, LANES), F32),
        ),
        in_specs=[anywhere] * 4,
        out_specs=(anywhere,) * 4,
        scratch_shapes=[
            dma((12,)), dma((2,)), dma((2, 8)), dma((2, 8, 4)), dma((2, 8, 4)), dma((2, 8, 4)), dma((2,)),
        ],
        compiler_params=pltpu.CompilerParams(collective_id=0, has_side_effects=True),
    )(x, dy, wq, wp)


def split(v):
    high = v.astype(BF16)
    return high, (v - high.astype(F32)).astype(BF16)


def mm(a, b, ca, cb):
    return lax.dot_general(a, b, (((ca,), (cb,)), ((), ())), preferred_element_type=F32)


def mm3(a, b, ca, cb):
    return mm(a[0], b[0], ca, cb) + (mm(a[1], b[0], ca, cb) + mm(a[0], b[1], ca, cb))


def compute_kernel(
    x_ref, dy_ref, wq_ref, wp_ref, gain_ref, bias_ref,
    out_ref, dx_ref, gq_ref, gp_ref, small_ref,
    xhat, rstd, nh, nl, yh, yl, wh, wl, ph, plo, qkv, da, ah, al, dh, dl,
):
    cols = [slice(LANES * j, LANES * (j + 1)) for j in range(9)]
    gain = gain_ref[...]
    bias = bias_ref[...]
    for j in range(9):
        wh[:, cols[j]], wl[:, cols[j]] = split(wq_ref[pl.ds(j, WIDTH, stride=9), :])
    for j in range(6):
        ph[:, cols[j]], plo[:, cols[j]] = split(wp_ref[pl.ds(j, HALF, stride=6), :])
    dy_sum = jnp.zeros((1, WIDTH), F32)
    for g in range(6):
        base = (g // 3) * 1152 + (g % 3) * 6
        rows = slice(64 * g, 64 * (g + 1))
        x = jnp.concatenate([x_ref[pl.ds(base + j, 64, stride=18), :] for j in range(6)], axis=1)
        centred = x - jnp.mean(x, axis=1, keepdims=True)
        r = lax.rsqrt(jnp.mean(centred * centred, axis=1, keepdims=True) + EPSILON)
        hat = centred * r
        xhat[rows, :] = hat
        rstd[rows, :] = jnp.broadcast_to(r, (64, LANES))
        nh[rows, :], nl[rows, :] = split(hat * gain + bias)
        y = jnp.concatenate([dy_ref[pl.ds(base + j, 64, stride=18), :] for j in range(6)], axis=1)
        yh[rows, :], yl[rows, :] = split(y)
        dy_sum = dy_sum + jnp.sum(y, axis=0, keepdims=True)
    for t in range(3):
        part = slice(HALF * t, HALF * (t + 1))
        qkv[:, part] = mm3((nh[...], nl[...]), (wh[:, part], wl[:, part]), 1, 0)
    da[...] = mm3((yh[...], yl[...]), (ph[...], plo[...]), 1, 1)
    left = lax.broadcasted_iota(jnp.int32, (LANES, LANES), 1) < 64
    row = lax.broadcasted_iota(jnp.int32, (2 * LANES, LANES), 0)
    col = lax.broadcasted_iota(jnp.int32, (2 * LANES, LANES), 1)
    same = ((row % LANES) < 64) == (col < 64)

    def stacked(v):
        return jnp.concatenate([jnp.where(left, v, 0.0), jnp.where(left, 0.0, v)], axis=0)

    def joined(v):
        return jnp.where(left, v[:LANES], v[LANES:])

    scale = 0.125
    for i in range(3):
        rows = slice(LANES * i, LANES * (i + 1))
        for h in range(3):
            q = split(stacked(qkv[rows, cols[h]] * scale))
            k = split(qkv[rows, cols[3 + h]])
            v = split(qkv[rows, cols[6 + h]])
            a = split(stacked(da[rows, cols[h]]))
            scores = jnp.where(same, mm3(q, k, 1, 1), -1e30)
            e = jnp.exp(scores - jnp.max(scores, axis=1, keepdims=True))
            probs = e / jnp.sum(e, axis=1, keepdims=True)
            pair = split(probs)
            ah[rows, cols[h]], al[rows, cols[h]] = split(joined(mm3(pair, v, 1, 0)))
            dh[rows, cols[6 + h]], dl[rows, cols[6 + h]] = split(mm3(pair, a, 0, 0))
            t = mm3(a, v, 1, 1) * probs
            ds = split(t - probs * jnp.sum(t, axis=1, keepdims=True))
            dh[rows, cols[h]], dl[rows, cols[h]] = split(joined(mm3(ds, k, 1, 0)) * scale)
            dh[rows, cols[3 + h]], dl[rows, cols[3 + h]] = split(mm3(ds, q, 0, 0))
    for t in range(2):
        part = slice(HALF * t, HALF * (t + 1))
        o = mm3((ah[...], al[...]), (ph[:, part], plo[:, part]), 1, 0)
        for g in range(6):
            for j in range(3):
                out_ref[pl.ds((g // 3) * 1152 + (g % 3) * 6 + 3 * t + j, 64, stride=18), :] = (
                    o[64 * g : 64 * (g + 1), cols[j]]
                )
        w = mm3((ah[...], al[...]), (yh[:, part], yl[:, part]), 0, 0)
        for j in range(3):
            gp_ref[pl.ds(3 * t + j, HALF, stride=6), :] = w[:, cols[j]]
    for t in range(3):
        part = slice(HALF * t, HALF * (t + 1))
        w = mm3((nh[...], nl[...]), (dh[:, part], dl[:, part]), 0, 0)
        for j in range(3):
            gq_ref[pl.ds(3 * t + j, WIDTH, stride=9), :] = w[:, cols[j]]
    gain_sum = jnp.zeros((1, WIDTH), F32)
    bias_sum = jnp.zeros((1, WIDTH), F32)
    for i in range(3):
        dn = mm3((dh[128 * i : 128 * (i + 1), :], dl[128 * i : 128 * (i + 1), :]), (wh[...], wl[...]), 1, 1)
        for half in range(2):
            g = 2 * i + half
            rows = slice(64 * g, 64 * (g + 1))
            n = dn[64 * half : 64 * (half + 1)]
            hat = xhat[rows, :]
            gain_sum = gain_sum + jnp.sum(n * hat, axis=0, keepdims=True)
            bias_sum = bias_sum + jnp.sum(n, axis=0, keepdims=True)
            n = n * gain
            m1 = jnp.mean(n, axis=1, keepdims=True)
            m2 = jnp.mean(n * hat, axis=1, keepdims=True)
            r = rstd[rows, 0:1]
            dx = r * (n - m1 - hat * m2)
            for j in range(6):
                dx_ref[pl.ds((g // 3) * 1152 + (g % 3) * 6 + j, 64, stride=18), :] = dx[:, cols[j]]
    for n, v in enumerate((gain_sum, bias_sum, dy_sum * 0.5)):
        for j in range(6):
            small_ref[6 * n + j : 6 * n + j + 1, :] = v[:, cols[j]]
    small_ref[18:24, :] = jnp.zeros((6, LANES), F32)


def compute(x, dy, wq, wp, gain, bias):
    vmem = pl.BlockSpec(memory_space=pltpu.VMEM)
    tokens = HALF
    return pl.pallas_call(
        compute_kernel,
        out_shape=(
            jax.ShapeDtypeStruct((2304, LANES), F32),
            jax.ShapeDtypeStruct((2304, LANES), F32),
            jax.ShapeDtypeStruct((6912, LANES), F32),
            jax.ShapeDtypeStruct((2304, LANES), F32),
            jax.ShapeDtypeStruct((24, LANES), F32),
        ),
        in_specs=[vmem] * 6,
        out_specs=(vmem,) * 5,
        scratch_shapes=[
            pltpu.VMEM((tokens, WIDTH), F32),
            pltpu.VMEM((tokens, LANES), F32),
            pltpu.VMEM((tokens, WIDTH), BF16),
            pltpu.VMEM((tokens, WIDTH), BF16),
            pltpu.VMEM((tokens, WIDTH), BF16),
            pltpu.VMEM((tokens, WIDTH), BF16),
            pltpu.VMEM((WIDTH, 3 * HALF), BF16),
            pltpu.VMEM((WIDTH, 3 * HALF), BF16),
            pltpu.VMEM((HALF, WIDTH), BF16),
            pltpu.VMEM((HALF, WIDTH), BF16),
            pltpu.VMEM((tokens, 3 * HALF), F32),
            pltpu.VMEM((tokens, HALF), F32),
            pltpu.VMEM((tokens, HALF), BF16),
            pltpu.VMEM((tokens, HALF), BF16),
            pltpu.VMEM((tokens, 3 * HALF), BF16),
            pltpu.VMEM((tokens, 3 * HALF), BF16),
        ],
        compiler_params=pltpu.CompilerParams(vmem_limit_bytes=50 * 1024 * 1024),
    )(x, dy, wq, wp, gain, bias)


RORDER = (4, 5, 3, 6, 2, 7, 1, 0)


def give_kernel(
    o_ref, dx_ref, gq_ref, gp_ref, sm_ref, of, df, rq, rp, so,
    ob, db, r1q, r1p, r2q, r2p, aq, ap, hq, hp, fq, fp, zq, zp, eq, ep, es, smx, smy, smz,
    ss, rb, r1, r2, rh, rf, rz, ro, ra, re,
):
    s, d, z, y, xh, xl, c = position()
    mirror, side, mate = others(s, d, xh, xl, c)
    corner = device(s, (1 - xl) * 2 + 1 - c)
    greet(s, d, z, y, xh, xl, c, corner)
    holds = lax.div(z, 4) == c
    oxh = 1 - xh
    mine_q, mine_p = pl.ds(27 * xl, 27), pl.ds(9 * xl, 9)
    yours_q, yours_p = pl.ds(27 * (1 - xl), 27), pl.ds(9 * (1 - xl), 9)

    def zdev(k):
        return device((lax.rem(z + k + 8, 8) * 4 + y) * 2 + xh, d)

    def ydev(k):
        return device((z * 4 + lax.rem(y + k, 4)) * 2 + xh, d)

    def row(k):
        return lax.rem(y + k, 4)

    def both(j, q_job, p_job):
        at = lax.rem(z + j, 8)
        q_job(at)

        @pl.when(lax.div(at, 4) == c)
        def _():
            p_job(lax.rem(at, 4))

    ROWS = (2, 1, 3, 0)

    def side_send(j):
        for k in ROWS:
            both(
                j,
                lambda at: send(gq_ref.at[at, row(k), oxh, yours_q], r1q.at[j, k], ss.at[0], r1.at[0, j, k], side),
                lambda at: send(gp_ref.at[at, row(k), oxh, yours_p], r1p.at[j, k], ss.at[1], r1.at[1, j, k], side),
            )

    def mirror_send(j):
        for k in ROWS:
            def q(at):
                wait_for(r1q.at[j, k], r1.at[0, j, k])
                r1q[j, k] = r1q[j, k] + gq_ref[at, row(k), oxh, mine_q]
                send(r1q.at[j, k], r2q.at[j, k], ss.at[5], r2.at[0, j, k], mirror)

            def p(at):
                wait_for(r1p.at[j, k], r1.at[1, j, k])
                r1p[j, k] = r1p[j, k] + gp_ref[at, row(k), oxh, mine_p]
                send(r1p.at[j, k], r2p.at[j, k], ss.at[6], r2.at[1, j, k], mirror)

            both(j, q, p)

    def gather(j, k):
        def q(at):
            wait_for(r2q.at[j, k], r2.at[0, j, k])
            aq[j, k, mine_q] = gq_ref[at, row(k), xh, mine_q]
            aq[j, k, yours_q] = gq_ref[at, row(k), xh, yours_q] + r2q[j, k]

        def p(at):
            wait_for(r2p.at[j, k], r2.at[1, j, k])
            ap[j, k, mine_p] = gp_ref[at, row(k), xh, mine_p]
            ap[j, k, yours_p] = gp_ref[at, row(k), xh, yours_p] + r2p[j, k]

        both(j, q, p)

    def y_far(j):
        gather(j, 2)
        for n, k in ((0, 1), (1, 3)):
            both(
                j,
                lambda at: send(aq.at[j, 2, pl.ds(27 * n, 27)], hq.at[j, n], ss.at[10], rh.at[0, j, n], ydev(k)),
                lambda at: send(ap.at[j, 2, pl.ds(9 * n, 9)], hp.at[j, n], ss.at[11], rh.at[1, j, n], ydev(k)),
            )

    def y_near(j):
        for n, k in ((0, 1), (1, 3)):
            gather(j, k)

            def q(at):
                wait_for(hq.at[j, n], rh.at[0, j, n])
                part = pl.ds(27 * n, 27)
                aq[j, k, part] = aq[j, k, part] + hq[j, n]
                send(aq.at[j, k], fq.at[j, n], ss.at[10], rf.at[0, j, n], ydev(k))

            def p(at):
                wait_for(hp.at[j, n], rh.at[1, j, n])
                part = pl.ds(9 * n, 9)
                ap[j, k, part] = ap[j, k, part] + hp[j, n]
                send(ap.at[j, k], fp.at[j, n], ss.at[11], rf.at[1, j, n], ydev(k))

            both(j, q, p)

    def z_step(j):
        gather(j, 0)

        def q(at):
            wait_for(fq.at[j, 0], rf.at[0, j, 0])
            wait_for(fq.at[j, 1], rf.at[0, j, 1])
            aq[j, 0] = aq[j, 0] + (fq[j, 0] + fq[j, 1])

        def p(at):
            wait_for(fp.at[j, 0], rf.at[1, j, 0])
            wait_for(fp.at[j, 1], rf.at[1, j, 1])
            ap[j, 0] = ap[j, 0] + (fp[j, 0] + fp[j, 1])

        both(j, q, p)

        def come(slot):
            def q(at):
                wait_for(zq.at[slot], rz.at[0, slot])
                aq[j, 0] = aq[j, 0] + zq[slot]

            def p(at):
                wait_for(zp.at[slot], rz.at[1, slot])
                ap[j, 0] = ap[j, 0] + zp[slot]

            both(j, q, p)

        def go(slot, k):
            both(
                j,
                lambda at: send(aq.at[j, 0], zq.at[slot], ss.at[13], rz.at[0, slot], zdev(k)),
                lambda at: send(ap.at[j, 0], zp.at[slot], ss.at[14], rz.at[1, slot], zdev(k)),
            )

        if j == 4:
            @pl.when(c == 0)
            def _():
                go(3, 1)

            @pl.when(c == 1)
            def _():
                go(5, -1)
        elif j == 0:
            come(0)
            come(8)
        else:
            if j in (3, 5):
                @pl.when(c == (0 if j == 3 else 1))
                def _():
                    come(j)
            else:
                come(j)
            if j < 4:
                go(j - 1, 1)
            else:
                go(j + 1, -1)

    def joined(n):
        own, buf, out = ((o_ref, ob, of), (dx_ref, db, df))[n]
        wait_for(buf, rb.at[n])

        def add(i, carry):
            at = pl.ds(8 * i, 8)
            buf[at] = buf[at] + own[c, at]
            return carry

        lax.fori_loop(0, 8, add, 0)
        pltpu.make_async_copy(buf.at[s], out.at[s], ro.at[n]).start()

    def spread(n, first, last):
        buf, out = ((ob, of), (db, df))[n]

        def one(k, carry):
            t = lax.rem(s + k, 64)
            send(buf.at[t], out.at[s], ss.at[7 + n], ro.at[n], device(t, d))
            return carry

        lax.fori_loop(first, last, one, 0)

    def small(step):
        if step == 0:
            smx[0] = sm_ref[...]
            send(smx.at[0], smx.at[1], ss.at[4], ra.at[0], mirror)
        if step == 1:
            wait_for(smx.at[1], ra.at[0])
            smy[y] = smx[0] + smx[1]
            for k in range(1, 4):
                send(smy.at[y], smy.at[y], ss.at[9], ra.at[1], ydev(k))
        if step == 2:
            wait_for(smy.at[pl.ds(0, 3)], ra.at[1])
            smz[z] = (smy[0] + smy[1]) + (smy[2] + smy[3])
            for k in range(1, 8):
                send(smz.at[z], smz.at[z], ss.at[12], ra.at[2], zdev(k))
        if step == 3:
            wait_for(smz.at[pl.ds(0, 7)], ra.at[2])
            es[d] = ((smz[0] + smz[1]) + (smz[2] + smz[3])) + ((smz[4] + smz[5]) + (smz[6] + smz[7]))
            for there in (side, mate, corner):
                send(es.at[d], es.at[d], ss.at[17], re.at[2], there)

    side_send(RORDER[0])
    send(o_ref.at[1 - c], ob, ss.at[2], rb.at[0], mate)
    send(dx_ref.at[1 - c], db, ss.at[3], rb.at[1], mate)
    side_send(RORDER[1])
    small(0)
    for t in range(1, 13):
        if t + 1 < 8:
            side_send(RORDER[t + 1])
        if 1 <= t < 9:
            mirror_send(RORDER[t - 1])
        if 2 <= t < 10:
            y_far(RORDER[t - 2])
        if 3 <= t < 11:
            y_near(RORDER[t - 3])
        if 4 <= t < 12:
            z_step(RORDER[t - 4])
        if t in (2, 4, 6):
            small(t // 2)
        if t == 1:
            joined(0)
        if t == 1:
            spread(0, 1, 17)
        if t == 2:
            spread(0, 17, 33)
        if t == 3:
            spread(0, 33, 49)
        if t == 4:
            spread(0, 49, 64)
        if t == 5:
            joined(1)
        if t == 5:
            spread(1, 1, 17)
        if t == 6:
            spread(1, 17, 33)
        if t == 7:
            spread(1, 33, 49)
        if t == 8:
            spread(1, 49, 64)

    eq[d] = aq[0, 0]
    for there in (side, mate, corner):
        send(eq.at[d], eq.at[d], ss.at[15], re.at[0], there)

    @pl.when(holds)
    def _():
        ep[xl] = ap[0, 0]
        for there in (side, mate, corner):
            send(ep.at[xl], ep.at[xl], ss.at[16], re.at[1], there)

    wait_for(es.at[pl.ds(0, 3)], re.at[2])
    so[...] = (es[0] + es[2]) + (es[1] + es[3])
    wait_for(eq.at[pl.ds(0, 3)], re.at[0])
    rq[0] = eq[0] + eq[2]
    rq[1] = eq[1] + eq[3]

    @pl.when(holds)
    def _():
        wait_for(ep.at[0], re.at[1])

    @pl.when(jnp.logical_not(holds))
    def _():
        wait_for(ep, re.at[1])

    rp[...] = ep[0] + ep[1]

    wait_for(ob, ro.at[0])
    wait_for(db, ro.at[1])
    wait_for(r1q, ss.at[0])
    wait_for(r1p.at[pl.ds(0, 4)], ss.at[1])
    wait_for(ob, ss.at[2])
    wait_for(db, ss.at[3])
    wait_for(smx.at[0], ss.at[4])
    wait_for(r2q, ss.at[5])
    wait_for(r2p.at[pl.ds(0, 4)], ss.at[6])
    wait_for(ob.at[pl.ds(0, 63)], ss.at[7])
    wait_for(db.at[pl.ds(0, 63)], ss.at[8])
    wait_for(smy.at[pl.ds(0, 3)], ss.at[9])
    wait_for(aq.at[:, pl.ds(0, 3)], ss.at[10])
    wait_for(ap.at[pl.ds(0, 4), pl.ds(0, 3)], ss.at[11])
    wait_for(smz.at[pl.ds(0, 7)], ss.at[12])
    wait_for(zq.at[pl.ds(0, 7)], ss.at[13])
    wait_for(eq.at[pl.ds(0, 3)], ss.at[15])
    wait_for(es.at[pl.ds(0, 3)], ss.at[17])

    @pl.when(holds)
    def _():
        wait_for(zp.at[pl.ds(0, 3)], ss.at[14])
        wait_for(zp.at[pl.ds(0, 3)], ss.at[16])

    @pl.when(jnp.logical_not(holds))
    def _():
        wait_for(zp.at[pl.ds(0, 4)], ss.at[14])


def give(o, dx, gq, gp, sm):
    dma = pltpu.SemaphoreType.DMA
    anywhere = pl.BlockSpec(memory_space=pl.ANY)
    vmem = pl.BlockSpec(memory_space=pltpu.VMEM)
    act = (64, 9, 2, LANES)
    q, p, sml = (54, 2, LANES), (18, 4, LANES), (24, LANES)
    q2, p2 = (27, 2, LANES), (9, 4, LANES)

    def buf(*shape):
        return pltpu.VMEM(shape, F32)

    return pl.pallas_call(
        give_kernel,
        out_shape=(
            jax.ShapeDtypeStruct(act, F32),
            jax.ShapeDtypeStruct(act, F32),
            jax.ShapeDtypeStruct((2,) + q, F32),
            jax.ShapeDtypeStruct(p, F32),
            jax.ShapeDtypeStruct(sml, F32),
        ),
        in_specs=[vmem] * 5,
        out_specs=(anywhere, anywhere, vmem, vmem, vmem),
        scratch_shapes=[
            buf(*act), buf(*act),
            buf(8, 4, *q2), buf(8, 4, *p2), buf(8, 4, *q2), buf(8, 4, *p2),
            buf(8, 4, *q), buf(8, 4, *p), buf(8, 2, *q2), buf(8, 2, *p2), buf(8, 2, *q), buf(8, 2, *p),
            buf(9, *q), buf(9, *p), buf(4, *q), buf(2, *p), buf(4, *sml),
            buf(2, *sml), buf(4, *sml), buf(8, *sml),
            dma((18,)), dma((2,)), dma((2, 8, 4)), dma((2, 8, 4)), dma((2, 8, 2)), dma((2, 8, 2)), dma((2, 9)),
            dma((2,)), dma((3,)), dma((3,)),
        ],
        compiler_params=pltpu.CompilerParams(
            collective_id=1, has_side_effects=True, vmem_limit_bytes=50 * 1024 * 1024
        ),
    )(o, dx, gq, gp, sm)


def on_device(
    frames, out_cotangent, layer_norm_gain, layer_norm_bias, qkv_weight, proj_weight, proj_bias
):
    c = lax.rem(lax.axis_index("dp"), 2)
    blocks = (64, 9, 2, LANES)
    half = lax.dynamic_index_in_dim(qkv_weight.reshape(12, 3, 2, HALF), c, axis=2, keepdims=False)
    x, dy, wq, wp = bring(
        frames.reshape(blocks),
        out_cotangent.reshape(blocks),
        half.reshape(54, 2, LANES),
        proj_weight.reshape(18, 4, LANES),
    )
    o, dx, gq, gp, small = compute(
        x.reshape(2304, LANES),
        dy.reshape(2304, LANES),
        wq.reshape(6912, LANES),
        wp.reshape(2304, LANES),
        layer_norm_gain.reshape(1, WIDTH),
        layer_norm_bias.reshape(1, WIDTH),
    )
    of, df, rq, rp, so = give(
        o.reshape((2,) + blocks),
        dx.reshape((2,) + blocks),
        gq.reshape(8, 4, 2, 54, 2, LANES),
        gp.reshape(4, 4, 2, 18, 4, LANES),
        small,
    )
    sums = so[:18].reshape(3, WIDTH)
    grad_qkv = jnp.transpose(rq.reshape(2, 12, 3, HALF), (1, 2, 0, 3)).reshape(12, 3 * WIDTH)
    return (
        frames + of.reshape(frames.shape) + proj_bias,
        out_cotangent + df.reshape(frames.shape),
        sums[0],
        sums[1],
        grad_qkv,
        rp.reshape(12, WIDTH),
        sums[2],
    )


def solution(mesh):
    return jax.shard_map(
        on_device,
        mesh=mesh,
        in_specs=(
            P("dp", "seq", None, None),
            P("dp", "seq", None, None),
            P(),
            P(),
            P("seq", None),
            P("seq", None),
            P(),
        ),
        out_specs=(
            P("dp", "seq", None, None),
            P("dp", "seq", None, None),
            P(),
            P(),
            P("seq", None),
            P("seq", None),
            P(),
        ),
        check_vma=False,
    )
```

time: 228 us -> 179 us (0.79)
  Pallas kernels: 213 us -> 164 us
    pallas_call x1, Pallas kernels: 103 us -> 70.3 us  [give(): pl.pallas_call(give_kernel, out_shape=(jax.ShapeDtypeStruct(act, F32), ja...]
    pallas_call x1, Pallas kernels: 83.1 us -> 67 us  [bring(): pl.pallas_call(bring_kernel, out_shape=(jax.ShapeDtypeStruct((2, 64, 9, 2...]
where the time goes in v2:
time: 179 us
  Pallas kernels  164 us (92%)
  local copies, waits for them, and re-layouts  12.5 us (7%)
    pallas_call x1, Pallas kernels, give(): pl.pallas_call(give_kernel, out_shape=(jax.ShapeDtypeStruct(act, F32), ja...  70.3 us
    pallas_call x1, Pallas kernels, bring(): pl.pallas_call(bring_kernel, out_shape=(jax.ShapeDtypeStruct((2, 64, 9, 2...  67 us
    pallas_call x1, Pallas kernels, compute(): pl.pallas_call(compute_kernel, out_shape=(jax.ShapeDtypeStruct((2304, LAN...  26.4 us

profile of v2, /device:TPU:1, one launch (start us, length us, event | category | flops | bytes accessed | tf_op | source)
XLA Modules:
  0.0 178.7 jit_solution(14183181706138908412)
XLA Ops:
  0.6 0.0 copy-start.2
  0.7 0.7 reshape.94.gain_ref
  1.4 0.7 reshape.95.bias_ref
  2.1 1.4 reshape.89.wp_ref
  3.5 1.0 reshape.87
  4.5 0.7 constant_dynamic-slice_fusion
  5.2 2.2 %reshape.85.x_ref = f32[64,9,2,128]{3,2,1,0:T(2,128)} reshape(f32[1,1,192,768]{3,2,1,0:T(8,128)} %param.7) | data formatting | bytes 1179648 | tf_op jit(solution)/shard_map/reshape | solution.py:773
  7.3 0.0 copy-done.2
  7.3 1.1 reshape.86.dy_ref
  8.5 67.0 %shard_map.126 = (f32[2,64,9,2,128]{4,3,2,1,0:T(2,128)}, f32[2,64,9,2,128]{4,3,2,1,0:T(2,128)}, f32[8,4,2,54,2,128]{5,4,3,2,1,0:T(2,128)}, f32[4,4,2,18,4,128]{5,4,3,2,1,0:T(4,128)}) custom-call(f32[64,9,2,128]{3,2,1,0:T(2,128)} %reshape.85.x_ref, f32[64,9,2,128]{3,2,1,0:T(2,128)} %reshape.86.dy_ref, f32[54,2,128]{2,1,0:T(2,128)} %bitcast.29, ...), custom_call_target="tpu_custom_call" | custom-call | tf_op jit(solution)/shard_map/pallas_call | solution.py:274
  75.4 26.4 %shard_map.127 = (f32[2304,128]{1,0:T(8,128)S(1)}, f32[2304,128]{1,0:T(8,128)S(1)}, f32[6912,128]{1,0:T(8,128)}, f32[2304,128]{1,0:T(8,128)S(1)}, f32[24,128]{1,0:T(8,128)S(1)}) custom-call(f32[2304,128]{1,0:T(8,128)} %bitcast.25, f32[2304,128]{1,0:T(8,128)} %bitcast.26, f32[6912,128]{1,0:T(8,128)} %bitcast.23, f32[2304,128]{1,0:T(8,128)} %bitcast.27, ...), custom_call_target="tpu_custom_call" | custom-call | tf_op jit(solution)/shard_map/pallas_call | solution.py:406
  101.8 0.0 copy-start
  101.8 1.0 copy-done
  102.9 70.3 %shard_map.128 = (f32[64,9,2,128]{3,2,1,0:T(2,128)S(1)}, f32[64,9,2,128]{3,2,1,0:T(2,128)S(1)}, f32[2,54,2,128]{3,2,1,0:T(2,128)S(1)}, f32[18,4,128]{2,1,0:T(4,128)S(1)}, f32[24,128]{1,0:T(8,128)S(1)}) custom-call(f32[2,64,9,2,128]{4,3,2,1,0:T(2,128)S(1)} %bitcast.20, f32[2,64,9,2,128]{4,3,2,1,0:T(2,128)S(1)} %bitcast.21, ...), custom_call_target="tpu_custom_call" | custom-call | tf_op jit(solution)/shard_map/pallas_call | solution.py:740
  173.2 0.0 copy-start.1
  173.2 0.0 copy-start.3
  173.2 0.5 reshape.100
  173.7 0.6 copy-done.1
  174.3 0.0 copy-done.3
  174.3 0.9 add_add_fusion
  175.1 0.6 slice_bitcast_fusion
  175.8 0.6 reshape.104
  176.4 0.1 reshape.102
  176.5 0.1 copy.18
  176.6 0.8 reshape.103
  177.3 0.5 reshape.101
  177.8 0.9 add.22
Async XLA Ops:
  0.6 6.7 %copy-start.2 = (f32[1,1,192,768]{3,2,1,0:T(8,128)S(1)}, f32[1,1,192,768]{3,2,1,0:T(8,128)}, u32[]{:S(2)}) copy-start(f32[1,1,192,768]{3,2,1,0:T(8,128)} %param.8) | copy-start | bytes 1769476
  101.8 1.0 copy-start
  173.2 1.1 copy-start.1
  173.2 1.1 copy-start.3

commit v3 on v2

v3 whole, which is shorter than its diff:
```python
import jax
import jax.numpy as jnp
from jax import lax
from jax.experimental import pallas as pl
from jax.experimental.pallas import tpu as pltpu
from jax.sharding import PartitionSpec as P

EPSILON = 1e-06
MESH = pl.DeviceIdType.MESH
F32 = jnp.float32
BF16 = jnp.bfloat16
WIDTH = 768
HALF = 384
LANES = 128


def position():
    s = lax.axis_index("seq")
    d = lax.axis_index("dp")
    return s, d, lax.div(s, 8), lax.rem(lax.div(s, 2), 4), lax.rem(s, 2), lax.div(d, 2), lax.rem(d, 2)


def device(s, d):
    return {"seq": s, "dp": d}


def greet(s, d, near):
    barrier = pltpu.get_barrier_semaphore()

    def one(k, carry):
        pl.semaphore_signal(barrier, inc=1, device_id=device(lax.rem(s + k, 64), d), device_id_type=MESH)
        return carry

    lax.fori_loop(1, 64, one, 0)
    for where in near:
        pl.semaphore_signal(barrier, inc=1, device_id=where, device_id_type=MESH)


def others(s, d, xh, xl, c):
    mirror = device(s + 1 - 2 * xh, (1 - xl) * 2 + c)
    side = device(s, (1 - xl) * 2 + c)
    mate = device(s, xl * 2 + 1 - c)
    return mirror, side, mate


def send(src, dst, send_sem, recv_sem, where):
    copy = pltpu.make_async_remote_copy(
        src_ref=src, dst_ref=dst, send_sem=send_sem, recv_sem=recv_sem, device_id=where, device_id_type=MESH
    )
    copy.start()


def wait_for(ref, sem):
    pltpu.make_async_copy(ref, ref, sem).wait()


def split(v):
    high = v.astype(BF16)
    return high, (v - high.astype(F32)).astype(BF16)


def mm(a, b, ca, cb):
    return lax.dot_general(a, b, (((ca,), (cb,)), ((), ())), preferred_element_type=F32)


def mm3(a, b, ca, cb):
    return mm(a[0], b[0], ca, cb) + (mm(a[1], b[0], ca, cb) + mm(a[0], b[1], ca, cb))


def stacked(left, v):
    return jnp.concatenate([jnp.where(left, v, 0.0), jnp.where(left, 0.0, v)], axis=0)


def joined_heads(left, v):
    return jnp.where(left, v[:LANES], v[LANES:])


ORDER = (0, 1, 7, 2, 6, 3, 5, 4)
RORDER = (4, 5, 3, 6, 2, 7, 1, 0)
ROWS = (2, 1, 3, 0)
COLS = [slice(LANES * j, LANES * (j + 1)) for j in range(9)]


def layer_kernel(
    x_ref, dy_ref, wq_raw, wp_raw, vec_ref, of, df, rq, rp, so,
    wq_own, wp_own, x2, dy2, wq2, wp2,
    xhat, rstd, nh, nl, yh, yl, wh, wl, ph, plo, qkv, da, ah, al, dh, dl, o2, d2, gq2, gp2, sm,
    ob, db, r1q, r1p, r2q, r2p, aq, ap, hq, hp, fq, fp, zq, zp, eq, ep, es, smx, smy, smz,
    ss, rx, rz, ry, rm, rs, rc, so_sem, rb, r1s, r2s, rh, rf, rzz, ro, ra, re,
):
    s, d, z, y, xh, xl, c = position()
    mirror, side, mate = others(s, d, xh, xl, c)
    corner = device(s, (1 - xl) * 2 + 1 - c)
    greet(s, d, (mirror, side, mate, corner))
    holds = lax.div(z, 4) == c
    for t in range(3):
        for n in range(3):
            at = pl.multiple_of(WIDTH * t + HALF * c + LANES * n, LANES)
            wq_own[pl.ds(3 * t + n, 12, stride=9), :] = wq_raw[:, pl.ds(at, LANES)]
    for n in range(6):
        wp_own[pl.ds(n, 12, stride=6), :] = wp_raw[:, COLS[n]]
    sm[...] = jnp.zeros((24, LANES), F32)
    wq_ref, wp_ref = wq_own.reshape(54, 2, LANES), wp_own.reshape(18, 4, LANES)
    xo, dyo = x2.reshape(2, 64, 9, 2, LANES), dy2.reshape(2, 64, 9, 2, LANES)
    o_ref, dx_ref = o2.reshape(2, 64, 9, 2, LANES), d2.reshape(2, 64, 9, 2, LANES)
    wqo, wpo = wq2.reshape(8, 4, 2, 54, 2, LANES), wp2.reshape(4, 4, 2, 18, 4, LANES)
    gq_ref, gp_ref = gq2.reshape(8, 4, 2, 54, 2, LANES), gp2.reshape(4, 4, 2, 18, 4, LANES)
    pl.semaphore_wait(pltpu.get_barrier_semaphore(), 67)

    def zdev(k):
        return device((lax.rem(z + k + 8, 8) * 4 + y) * 2 + xh, d)

    def ydev(k):
        return device((z * 4 + lax.rem(y + k, 4)) * 2 + xh, d)

    def both(j, q_job, p_job):
        at = lax.rem(z + j, 8)
        q_job(at)

        @pl.when(lax.div(at, 4) == c)
        def _():
            p_job(lax.rem(at, 4))

    def along_z(j, to, there, src_q=None, src_p=None):
        both(
            j,
            lambda at: send(wqo.at[at, y, xh] if src_q is None else src_q, wqo.at[at, y, xh], ss.at[0], rz.at[0, to], there),
            lambda at: send(wpo.at[at, y, xh] if src_p is None else src_p, wpo.at[at, y, xh], ss.at[1], rz.at[1, to], there),
        )

    def z_stage(j):
        if j == 0:
            along_z(0, 7, zdev(1), wq_ref, wp_ref)
            along_z(0, 1, zdev(-1), wq_ref, wp_ref)
            both(
                0,
                lambda at: pltpu.make_async_copy(wq_ref, wqo.at[at, y, xh], rz.at[0, 0]).start(),
                lambda at: pltpu.make_async_copy(wp_ref, wpo.at[at, y, xh], rz.at[1, 0]).start(),
            )
        both(
            j,
            lambda at: wait_for(wqo.at[at, y, xh], rz.at[0, j]),
            lambda at: wait_for(wpo.at[at, y, xh], rz.at[1, j]),
        )
        if j in (7, 6):
            along_z(j, j - 1, zdev(1))
        if j in (1, 2):
            along_z(j, j + 1, zdev(-1))
        if j == 5:
            @pl.when(c == 0)
            def _():
                along_z(5, 4, zdev(1))
        if j == 3:
            @pl.when(c == 1)
            def _():
                along_z(3, 4, zdev(-1))

    def y_send(j):
        for k in (1, 3):
            both(
                j,
                lambda at: send(wqo.at[at, y, xh], wqo.at[at, y, xh], ss.at[4], ry.at[0, j, k], ydev(k)),
                lambda at: send(wpo.at[at, y, xh], wpo.at[at, y, xh], ss.at[5], ry.at[1, j, k], ydev(k)),
            )

    def across(j, k):
        row = lax.rem(y + 4 - k, 4)
        hq, hp = pl.ds(27 * (1 - xl), 27), pl.ds(9 * (1 - xl), 9)

        def q(at):
            ref = wqo.at[at, row, xh, hq]
            send(ref, ref, ss.at[6], rm.at[0, j, row], mirror)

        def p(at):
            ref = wpo.at[at, row, xh, hp]
            send(ref, ref, ss.at[7], rm.at[1, j, row], mirror)

        both(j, q, p)

    def y_wait(j, k):
        row = lax.rem(y + 4 - k, 4)
        both(
            j,
            lambda at: wait_for(wqo.at[at, row, xh], ry.at[0, j, k]),
            lambda at: wait_for(wpo.at[at, row, xh], ry.at[1, j, k]),
        )

    def y_pass(j, k):
        h = 0 if k == 1 else 1
        row = lax.rem(y + 4 - k, 4)

        def q(at):
            ref = wqo.at[at, row, xh, pl.ds(27 * h, 27)]
            send(ref, ref, ss.at[4], ry.at[0, j, 2], ydev(k))

        def p(at):
            ref = wpo.at[at, row, xh, pl.ds(9 * h, 9)]
            send(ref, ref, ss.at[5], ry.at[1, j, 2], ydev(k))

        both(j, q, p)

    def forward(j, k):
        row = lax.rem(y + 4 - k, 4)
        hq, hp = pl.ds(27 * xl, 27), pl.ds(9 * xl, 9)

        def q(at):
            ref = wqo.at[at, row, 1 - xh, hq]
            wait_for(ref, rm.at[0, j, row])
            send(ref, ref, ss.at[8], rs.at[0, j, row], side)

        def p(at):
            ref = wpo.at[at, row, 1 - xh, hp]
            wait_for(ref, rm.at[1, j, row])
            send(ref, ref, ss.at[9], rs.at[1, j, row], side)

        both(j, q, p)

    pltpu.make_async_copy(x_ref.at[s], xo.at[c, s], rx.at[0]).start()
    pltpu.make_async_copy(dy_ref.at[s], dyo.at[c, s], rx.at[1]).start()

    def spread_in(n, first, last):
        src, dst = ((x_ref, xo), (dy_ref, dyo))[n]

        def one(k, carry):
            t = lax.rem(s + k, 64)
            send(src.at[t], dst.at[c, s], ss.at[2 + n], rx.at[n], device(t, d))
            return carry

        lax.fori_loop(first, last, one, 0)

    gain = vec_ref[0:1, :]
    bias = vec_ref[1:2, :]

    def weights(j):
        at = lax.rem(z + j, 8)
        for k in range(4):
            row = lax.rem(y + 4 - k, 4)
            both(
                j,
                lambda at: wait_for(wqo.at[at, row, 1 - xh, pl.ds(27 * (1 - xl), 27)], rs.at[0, j, row]),
                lambda at: wait_for(wpo.at[at, row, 1 - xh, pl.ds(9 * (1 - xl), 9)], rs.at[1, j, row]),
            )

        def q(at):
            rows = pl.ds(pl.multiple_of(at * 96, 96), 96)
            for n in range(9):
                wh[rows, COLS[n]], wl[rows, COLS[n]] = split(wq2[pl.ds(at * 864 + n, 96, stride=9), :])

        def p(at):
            rows = pl.ds(pl.multiple_of(at * 96, 96), 96)
            for n in range(6):
                ph[rows, COLS[n]], plo[rows, COLS[n]] = split(wp2[pl.ds(at * 576 + n, 96, stride=6), :])

        both(j, q, p)

    def tokens(ref, g):
        base = (g // 3) * 1152 + (g % 3) * 6
        return jnp.concatenate([ref[pl.ds(base + n, 64, stride=18), :] for n in range(6)], axis=1)

    def norm(g):
        rows = slice(64 * g, 64 * (g + 1))
        v = tokens(x2, g)
        centred = v - jnp.mean(v, axis=1, keepdims=True)
        r = lax.rsqrt(jnp.mean(centred * centred, axis=1, keepdims=True) + EPSILON)
        hat = centred * r
        xhat[rows, :] = hat
        rstd[rows, :] = jnp.broadcast_to(r, (64, LANES))
        nh[rows, :], nl[rows, :] = split(hat * gain + bias)

    def cotangent(g):
        rows = slice(64 * g, 64 * (g + 1))
        v = tokens(dy2, g)
        yh[rows, :], yl[rows, :] = split(v)
        add_small(12, jnp.sum(v, axis=0, keepdims=True) * 0.5)

    def add_small(first, v):
        for n in range(6):
            at = slice(first + n, first + n + 1)
            sm[at, :] = sm[at, :] + v[:, COLS[n]]

    def attention():
        left = lax.broadcasted_iota(jnp.int32, (LANES, LANES), 1) < 64
        row = lax.broadcasted_iota(jnp.int32, (2 * LANES, LANES), 0)
        col = lax.broadcasted_iota(jnp.int32, (2 * LANES, LANES), 1)
        same = ((row % LANES) < 64) == (col < 64)
        scale = 0.125
        for i in range(3):
            rows = slice(LANES * i, LANES * (i + 1))
            for h in range(3):
                q = split(stacked(left, qkv[rows, COLS[h]] * scale))
                k = split(qkv[rows, COLS[3 + h]])
                v = split(qkv[rows, COLS[6 + h]])
                a = split(stacked(left, da[rows, COLS[h]]))
                scores = jnp.where(same, mm3(q, k, 1, 1), -1e30)
                e = jnp.exp(scores - jnp.max(scores, axis=1, keepdims=True))
                probs = e / jnp.sum(e, axis=1, keepdims=True)
                pair = split(probs)
                ah[rows, COLS[h]], al[rows, COLS[h]] = split(joined_heads(left, mm3(pair, v, 1, 0)))
                dh[rows, COLS[6 + h]], dl[rows, COLS[6 + h]] = split(mm3(pair, a, 0, 0))
                t = mm3(a, v, 1, 1) * probs
                ds = split(t - probs * jnp.sum(t, axis=1, keepdims=True))
                dh[rows, COLS[h]], dl[rows, COLS[h]] = split(joined_heads(left, mm3(ds, k, 1, 0)) * scale)
                dh[rows, COLS[3 + h]], dl[rows, COLS[3 + h]] = split(mm3(ds, q, 0, 0))

    def project(t):
        part = slice(HALF * t, HALF * (t + 1))
        o = mm3((ah[...], al[...]), (ph[:, part], plo[:, part]), 1, 0)
        for g in range(6):
            for n in range(3):
                o2[pl.ds((g // 3) * 1152 + (g % 3) * 6 + 3 * t + n, 64, stride=18), :] = (
                    o[64 * g : 64 * (g + 1), COLS[n]]
                )

    def grad_proj(t):
        part = slice(HALF * t, HALF * (t + 1))
        w = mm3((ah[...], al[...]), (yh[:, part], yl[:, part]), 0, 0)
        for n in range(3):
            gp2[pl.ds(3 * t + n, HALF, stride=6), :] = w[:, COLS[n]]

    def grad_qkv(t):
        part = slice(HALF * t, HALF * (t + 1))
        w = mm3((nh[...], nl[...]), (dh[:, part], dl[:, part]), 0, 0)
        for n in range(3):
            gq2[pl.ds(3 * t + n, WIDTH, stride=9), :] = w[:, COLS[n]]

    def grad_input(i):
        dn = mm3((dh[128 * i : 128 * (i + 1), :], dl[128 * i : 128 * (i + 1), :]), (wh[...], wl[...]), 1, 1)
        for half in range(2):
            g = 2 * i + half
            rows = slice(64 * g, 64 * (g + 1))
            n = dn[64 * half : 64 * (half + 1)]
            hat = xhat[rows, :]
            add_small(0, jnp.sum(n * hat, axis=0, keepdims=True))
            add_small(6, jnp.sum(n, axis=0, keepdims=True))
            n = n * gain
            m1 = jnp.mean(n, axis=1, keepdims=True)
            m2 = jnp.mean(n * hat, axis=1, keepdims=True)
            dx = rstd[rows, 0:1] * (n - m1 - hat * m2)
            for j in range(6):
                d2[pl.ds((g // 3) * 1152 + (g % 3) * 6 + j, 64, stride=18), :] = dx[:, COLS[j]]

    oxh = 1 - xh
    mine_q, mine_p = pl.ds(27 * xl, 27), pl.ds(9 * xl, 9)
    yours_q, yours_p = pl.ds(27 * (1 - xl), 27), pl.ds(9 * (1 - xl), 9)

    def row(k):
        return lax.rem(y + k, 4)

    def side_send(j):
        for k in ROWS:
            both(
                j,
                lambda at: send(gq_ref.at[at, row(k), oxh, yours_q], r1q.at[j, k], so_sem.at[0], r1s.at[0, j, k], side),
                lambda at: send(gp_ref.at[at, row(k), oxh, yours_p], r1p.at[j, k], so_sem.at[1], r1s.at[1, j, k], side),
            )

    def mirror_send(j):
        for k in ROWS:
            def q(at):
                wait_for(r1q.at[j, k], r1s.at[0, j, k])
                r1q[j, k] = r1q[j, k] + gq_ref[at, row(k), oxh, mine_q]
                send(r1q.at[j, k], r2q.at[j, k], so_sem.at[5], r2s.at[0, j, k], mirror)

            def p(at):
                wait_for(r1p.at[j, k], r1s.at[1, j, k])
                r1p[j, k] = r1p[j, k] + gp_ref[at, row(k), oxh, mine_p]
                send(r1p.at[j, k], r2p.at[j, k], so_sem.at[6], r2s.at[1, j, k], mirror)

            both(j, q, p)

    def gather(j, k):
        def q(at):
            wait_for(r2q.at[j, k], r2s.at[0, j, k])
            aq[j, k, mine_q] = gq_ref[at, row(k), xh, mine_q]
            aq[j, k, yours_q] = gq_ref[at, row(k), xh, yours_q] + r2q[j, k]

        def p(at):
            wait_for(r2p.at[j, k], r2s.at[1, j, k])
            ap[j, k, mine_p] = gp_ref[at, row(k), xh, mine_p]
            ap[j, k, yours_p] = gp_ref[at, row(k), xh, yours_p] + r2p[j, k]

        both(j, q, p)

    def y_far(j):
        gather(j, 2)
        for n, k in ((0, 1), (1, 3)):
            both(
                j,
                lambda at: send(aq.at[j, 2, pl.ds(27 * n, 27)], hq.at[j, n], so_sem.at[10], rh.at[0, j, n], ydev(k)),
                lambda at: send(ap.at[j, 2, pl.ds(9 * n, 9)], hp.at[j, n], so_sem.at[11], rh.at[1, j, n], ydev(k)),
            )

    def y_near(j):
        for n, k in ((0, 1), (1, 3)):
            gather(j, k)

            def q(at):
                wait_for(hq.at[j, n], rh.at[0, j, n])
                part = pl.ds(27 * n, 27)
                aq[j, k, part] = aq[j, k, part] + hq[j, n]
                send(aq.at[j, k], fq.at[j, n], so_sem.at[10], rf.at[0, j, n], ydev(k))

            def p(at):
                wait_for(hp.at[j, n], rh.at[1, j, n])
                part = pl.ds(9 * n, 9)
                ap[j, k, part] = ap[j, k, part] + hp[j, n]
                send(ap.at[j, k], fp.at[j, n], so_sem.at[11], rf.at[1, j, n], ydev(k))

            both(j, q, p)

    def z_step(j):
        gather(j, 0)

        def q(at):
            wait_for(fq.at[j, 0], rf.at[0, j, 0])
            wait_for(fq.at[j, 1], rf.at[0, j, 1])
            aq[j, 0] = aq[j, 0] + (fq[j, 0] + fq[j, 1])

        def p(at):
            wait_for(fp.at[j, 0], rf.at[1, j, 0])
            wait_for(fp.at[j, 1], rf.at[1, j, 1])
            ap[j, 0] = ap[j, 0] + (fp[j, 0] + fp[j, 1])

        both(j, q, p)

        def come(slot):
            def q(at):
                wait_for(zq.at[slot], rzz.at[0, slot])
                aq[j, 0] = aq[j, 0] + zq[slot]

            def p(at):
                wait_for(zp.at[slot], rzz.at[1, slot])
                ap[j, 0] = ap[j, 0] + zp[slot]

            both(j, q, p)

        def go(slot, k):
            both(
                j,
                lambda at: send(aq.at[j, 0], zq.at[slot], so_sem.at[13], rzz.at[0, slot], zdev(k)),
                lambda at: send(ap.at[j, 0], zp.at[slot], so_sem.at[14], rzz.at[1, slot], zdev(k)),
            )

        if j == 4:
            @pl.when(c == 0)
            def _():
                go(3, 1)

            @pl.when(c == 1)
            def _():
                go(5, -1)
        elif j == 0:
            come(0)
            come(8)
        else:
            if j in (3, 5):
                @pl.when(c == (0 if j == 3 else 1))
                def _():
                    come(j)
            else:
                come(j)
            if j < 4:
                go(j - 1, 1)
            else:
                go(j + 1, -1)

    def joined(n):
        own, buf, out = ((o_ref, ob, of), (dx_ref, db, df))[n]
        wait_for(buf, rb.at[n])

        def add(i, carry):
            at = pl.ds(8 * i, 8)
            buf[at] = buf[at] + own[c, at]
            return carry

        lax.fori_loop(0, 8, add, 0)
        pltpu.make_async_copy(buf.at[s], out.at[s], ro.at[n]).start()

    def spread(n, first, last):
        buf, out = ((ob, of), (db, df))[n]

        def one(k, carry):
            t = lax.rem(s + k, 64)
            send(buf.at[t], out.at[s], so_sem.at[7 + n], ro.at[n], device(t, d))
            return carry

        lax.fori_loop(first, last, one, 0)

    def small(step):
        if step == 0:
            smx[0] = sm[...]
            send(smx.at[0], smx.at[1], so_sem.at[4], ra.at[0], mirror)
        if step == 1:
            wait_for(smx.at[1], ra.at[0])
            smy[y] = smx[0] + smx[1]
            for k in range(1, 4):
                send(smy.at[y], smy.at[y], so_sem.at[9], ra.at[1], ydev(k))
        if step == 2:
            wait_for(smy.at[pl.ds(0, 3)], ra.at[1])
            smz[z] = (smy[0] + smy[1]) + (smy[2] + smy[3])
            for k in range(1, 8):
                send(smz.at[z], smz.at[z], so_sem.at[12], ra.at[2], zdev(k))
        if step == 3:
            wait_for(smz.at[pl.ds(0, 7)], ra.at[2])
            es[d] = ((smz[0] + smz[1]) + (smz[2] + smz[3])) + ((smz[4] + smz[5]) + (smz[6] + smz[7]))
            for there in (side, mate, corner):
                send(es.at[d], es.at[d], so_sem.at[17], re.at[2], there)

    for t in range(14):
        if t < 8:
            z_stage(ORDER[t])
            y_send(ORDER[t])
            across(ORDER[t], 0)
        if 1 <= t < 9:
            j = ORDER[t - 1]
            for k in (1, 3):
                y_wait(j, k)
                y_pass(j, k)
                across(j, k)
        if 2 <= t < 10:
            j = ORDER[t - 2]
            y_wait(j, 2)
            across(j, 2)
            forward(j, 0)
        if 3 <= t < 11:
            j = ORDER[t - 3]
            for k in (1, 3, 2):
                forward(j, k)
        if 1 <= t <= 4:
            spread_in(0, 16 * t - 15, min(64, 16 * t + 1))
        if 5 <= t <= 8:
            spread_in(1, 16 * t - 79, min(64, 16 * t - 63))
        if t == 10:
            wait_for(xo.at[c], rx.at[0])
            send(xo.at[c], xo.at[c], ss.at[10], rc.at[0], mate)
        if t == 11:
            wait_for(dyo.at[c], rx.at[1])
            send(dyo.at[c], dyo.at[c], ss.at[11], rc.at[1], mate)
        if 6 <= t < 14:
            weights(ORDER[t - 6])
        if t == 12:
            wait_for(xo.at[1 - c], rc.at[0])
            for g in range(6):
                norm(g)
        if t == 13:
            wait_for(dyo.at[1 - c], rc.at[1])
            for g in range(6):
                cotangent(g)

    for t in range(3):
        part = slice(HALF * t, HALF * (t + 1))
        qkv[:, part] = mm3((nh[...], nl[...]), (wh[:, part], wl[:, part]), 1, 0)
    da[...] = mm3((yh[...], yl[...]), (ph[...], plo[...]), 1, 1)
    attention()
    for t in range(3):
        grad_qkv(t)
    for t in range(2):
        grad_proj(t)

    side_send(RORDER[0])
    side_send(RORDER[1])
    for t in range(1, 13):
        if t + 1 < 8:
            side_send(RORDER[t + 1])
        if t == 1:
            project(0)
        if 1 <= t < 9:
            mirror_send(RORDER[t - 1])
        if t == 1:
            project(1)
            send(o_ref.at[1 - c], ob, so_sem.at[2], rb.at[0], mate)
        if 2 <= t < 10:
            y_far(RORDER[t - 2])
        if t in (2, 3, 4):
            grad_input(t - 2)
        if t == 4:
            send(dx_ref.at[1 - c], db, so_sem.at[3], rb.at[1], mate)
            small(0)
        if 3 <= t < 11:
            y_near(RORDER[t - 3])
        if 4 <= t < 12:
            z_step(RORDER[t - 4])
        if t in (6, 8, 10):
            small(t // 2 - 2)
        if t == 2:
            joined(0)
        if 2 <= t <= 5:
            spread(0, 16 * t - 31, min(64, 16 * t - 15))
        if t == 5:
            joined(1)
        if 6 <= t <= 9:
            spread(1, 16 * t - 95, min(64, 16 * t - 79))

    eq[d] = aq[0, 0]
    for there in (side, mate, corner):
        send(eq.at[d], eq.at[d], so_sem.at[15], re.at[0], there)

    @pl.when(holds)
    def _():
        ep[xl] = ap[0, 0]
        for there in (side, mate, corner):
            send(ep.at[xl], ep.at[xl], so_sem.at[16], re.at[1], there)

    wait_for(es.at[pl.ds(0, 3)], re.at[2])
    so[...] = (es[0] + es[2]) + (es[1] + es[3])
    wait_for(eq.at[pl.ds(0, 3)], re.at[0])
    rq[0] = eq[0] + eq[2]
    rq[1] = eq[1] + eq[3]

    @pl.when(holds)
    def _():
        wait_for(ep.at[0], re.at[1])

    @pl.when(jnp.logical_not(holds))
    def _():
        wait_for(ep, re.at[1])

    rp[...] = ep[0] + ep[1]

    wait_for(ob, ro.at[0])
    wait_for(db, ro.at[1])
    wait_for(r1q, so_sem.at[0])
    wait_for(r1p.at[pl.ds(0, 4)], so_sem.at[1])
    wait_for(ob, so_sem.at[2])
    wait_for(db, so_sem.at[3])
    wait_for(smx.at[0], so_sem.at[4])
    wait_for(r2q, so_sem.at[5])
    wait_for(r2p.at[pl.ds(0, 4)], so_sem.at[6])
    wait_for(ob.at[pl.ds(0, 63)], so_sem.at[7])
    wait_for(db.at[pl.ds(0, 63)], so_sem.at[8])
    wait_for(smy.at[pl.ds(0, 3)], so_sem.at[9])
    wait_for(aq.at[:, pl.ds(0, 3)], so_sem.at[10])
    wait_for(ap.at[pl.ds(0, 4), pl.ds(0, 3)], so_sem.at[11])
    wait_for(smz.at[pl.ds(0, 7)], so_sem.at[12])
    wait_for(zq.at[pl.ds(0, 7)], so_sem.at[13])
    wait_for(eq.at[pl.ds(0, 3)], so_sem.at[15])
    wait_for(es.at[pl.ds(0, 3)], so_sem.at[17])

    @pl.when(holds)
    def _():
        wait_for(zp.at[pl.ds(0, 3)], so_sem.at[14])
        wait_for(zp.at[pl.ds(0, 3)], so_sem.at[16])

    @pl.when(jnp.logical_not(holds))
    def _():
        wait_for(zp.at[pl.ds(0, 4)], so_sem.at[14])
    wait_for(wqo.at[pl.ds(0, 7), 0, 0], ss.at[0])
    z_sends = (0, 7, 6, 0, 1, 2)
    for j in z_sends:
        @pl.when(lax.div(lax.rem(z + j, 8), 4) == c)
        def _():
            wait_for(wp_ref, ss.at[1])
    for j, core in ((5, 0), (3, 1)):
        @pl.when(jnp.logical_and(c == core, lax.div(lax.rem(z + j, 8), 4) == c))
        def _():
            wait_for(wp_ref, ss.at[1])
    wait_for(xo.at[0, pl.ds(0, 63)], ss.at[2])
    wait_for(xo.at[0, pl.ds(0, 63)], ss.at[3])
    wait_for(wqo.at[:, pl.ds(0, 3), 0], ss.at[4])
    wait_for(wpo.at[:, pl.ds(0, 3), 0], ss.at[5])
    for sem in (6, 8):
        wait_for(wqo.at[:, :, 0, pl.ds(0, 27)], ss.at[sem])
    for sem in (7, 9):
        wait_for(wpo.at[:, :, 0, pl.ds(0, 9)], ss.at[sem])
    wait_for(xo.at[0], ss.at[10])
    wait_for(xo.at[0], ss.at[11])


def layer(x, dy, wq, wp, vectors):
    dma = pltpu.SemaphoreType.DMA
    anywhere = pl.BlockSpec(memory_space=pl.ANY)
    vmem = pl.BlockSpec(memory_space=pltpu.VMEM)
    act, sml = (64, 9, 2, LANES), (24, LANES)
    q, p = (54, 2, LANES), (18, 4, LANES)
    q2, p2 = (27, 2, LANES), (9, 4, LANES)
    n = HALF

    def buf(*shape):
        return pltpu.VMEM(shape, F32)

    def low(*shape):
        return pltpu.VMEM(shape, BF16)

    return pl.pallas_call(
        layer_kernel,
        out_shape=(
            jax.ShapeDtypeStruct(act, F32),
            jax.ShapeDtypeStruct(act, F32),
            jax.ShapeDtypeStruct((2,) + q, F32),
            jax.ShapeDtypeStruct(p, F32),
            jax.ShapeDtypeStruct(sml, F32),
        ),
        in_specs=[anywhere, anywhere, vmem, vmem, vmem],
        out_specs=(anywhere, anywhere, vmem, vmem, vmem),
        scratch_shapes=[
            buf(108, LANES), buf(72, LANES),
            buf(2304, LANES), buf(2304, LANES), buf(6912, LANES), buf(2304, LANES),
            buf(n, WIDTH), buf(n, LANES), low(n, WIDTH), low(n, WIDTH), low(n, WIDTH), low(n, WIDTH),
            low(WIDTH, 3 * HALF), low(WIDTH, 3 * HALF), low(HALF, WIDTH), low(HALF, WIDTH),
            buf(n, 3 * HALF), buf(n, HALF), low(n, HALF), low(n, HALF), low(n, 3 * HALF), low(n, 3 * HALF),
            buf(2304, LANES), buf(2304, LANES), buf(6912, LANES), buf(2304, LANES), buf(*sml),
            buf(*act), buf(*act),
            buf(8, 4, *q2), buf(8, 4, *p2), buf(8, 4, *q2), buf(8, 4, *p2),
            buf(8, 4, *q), buf(8, 4, *p), buf(8, 2, *q2), buf(8, 2, *p2), buf(8, 2, *q), buf(8, 2, *p),
            buf(9, *q), buf(9, *p), buf(4, *q), buf(2, *p), buf(4, *sml),
            buf(2, *sml), buf(4, *sml), buf(8, *sml),
            dma((12,)), dma((2,)), dma((2, 8)), dma((2, 8, 4)), dma((2, 8, 4)), dma((2, 8, 4)), dma((2,)),
            dma((18,)), dma((2,)), dma((2, 8, 4)), dma((2, 8, 4)), dma((2, 8, 2)), dma((2, 8, 2)), dma((2, 9)),
            dma((2,)), dma((3,)), dma((3,)),
        ],
        compiler_params=pltpu.CompilerParams(
            collective_id=0, has_side_effects=True, vmem_limit_bytes=56 * 1024 * 1024
        ),
    )(x, dy, wq, wp, vectors)


def on_device(
    frames, out_cotangent, layer_norm_gain, layer_norm_bias, qkv_weight, proj_weight, proj_bias
):
    blocks = (64, 9, 2, LANES)
    of, df, rq, rp, so = layer(
        frames.reshape(blocks),
        out_cotangent.reshape(blocks),
        qkv_weight,
        proj_weight,
        jnp.stack([layer_norm_gain, layer_norm_bias]),
    )
    sums = so[:18].reshape(3, WIDTH)
    grad_qkv = jnp.transpose(rq.reshape(2, 12, 3, HALF), (1, 2, 0, 3)).reshape(12, 3 * WIDTH)
    return (
        frames + of.reshape(frames.shape) + proj_bias,
        out_cotangent + df.reshape(frames.shape),
        sums[0],
        sums[1],
        grad_qkv,
        rp.reshape(12, WIDTH),
        sums[2],
    )


def solution(mesh):
    return jax.shard_map(
        on_device,
        mesh=mesh,
        in_specs=(
            P("dp", "seq", None, None),
            P("dp", "seq", None, None),
            P(),
            P(),
            P("seq", None),
            P("seq", None),
            P(),
        ),
        out_specs=(
            P("dp", "seq", None, None),
            P("dp", "seq", None, None),
            P(),
            P(),
            P("seq", None),
            P("seq", None),
            P(),
        ),
        check_vma=False,
    )
```

time: 179 us -> 155 us (0.87)
  Pallas kernels: 164 us -> 143 us
  local copies, waits for them, and re-layouts: 12.5 us -> 8.3 us
    pallas_call x3 -> x1, Pallas kernels: 164 us -> 143 us  [layer(): pl.pallas_call(layer_kernel, out_shape=(jax.ShapeDtypeStruct(act, F32), j...]
    reshape x4 -> x0, local copies, waits for them, and re-layouts: 3.84 us -> none  [the longest x1 1.43 us: on_device(): proj_weight.reshape(18, 4, LANES)]
where the time goes in v3:
time: 155 us; the launch traced here: 154 us
  Pallas kernels  143 us (92%)
  local copies, waits for them, and re-layouts  8.3 us (5%)
  other arithmetic  2.36 us (2%)
    pallas_call x1, Pallas kernels, layer(): pl.pallas_call(layer_kernel, out_shape=(jax.ShapeDtypeStruct(act, F32), j...  143 us

profile of v3, /device:TPU:1, one launch (start us, length us, event | category | flops | bytes accessed | tf_op | source)
XLA Modules:
  0.0 154.2 jit_solution(17897421939536610905)
XLA Ops:
  0.6 0.0 copy-start.7
  0.6 0.7 stack.9
  1.3 0.0 copy-done.7
  1.3 0.6 pad_maximum_fusion.vec_ref
  2.0 0.0 copy-start.1
  2.0 2.2 %reshape.45.x_ref = f32[64,9,2,128]{3,2,1,0:T(2,128)} reshape(f32[1,1,192,768]{3,2,1,0:T(8,128)} %param.7) | data formatting | bytes 1179648 | tf_op jit(solution)/shard_map/reshape | solution.py:722
  4.2 0.0 copy-done.1
  4.2 1.1 reshape.46.dy_ref
  5.3 142.8 %shard_map.126 = (f32[64,9,2,128]{3,2,1,0:T(2,128)}, f32[64,9,2,128]{3,2,1,0:T(2,128)}, f32[2,54,2,128]{3,2,1,0:T(2,128)}, f32[18,4,128]{2,1,0:T(4,128)}, f32[24,128]{1,0:T(8,128)}) custom-call(f32[64,9,2,128]{3,2,1,0:T(2,128)} %reshape.45.x_ref, f32[64,9,2,128]{3,2,1,0:T(2,128)} %reshape.46.dy_ref, f32[12,2304]{1,0:T(8,128)} %wq_raw.1, f32[12,768]{1,0:T(8,128)} %wp_raw.1, ...), custom_call_target="tpu_custom_call" | custom-call | tf_op jit(solution)/shard_map/pallas_call | solution.py:684
  148.1 0.0 copy-start
  148.1 0.0 copy-start.6
  148.1 1.6 %reshape.47 = f32[1,1,192,768]{3,2,1,0:T(8,128)S(1)} reshape(f32[64,9,2,128]{3,2,1,0:T(2,128)} %get-tuple-element.12) | data formatting | bytes 1179648 | tf_op jit(solution)/shard_map/reshape | solution.py:731
  149.7 0.0 copy-done
  149.7 0.0 copy-done.6
  149.7 0.0 copy-start.5
  149.8 0.0 copy-start.4
  149.8 0.0 copy-start.3
  149.8 0.9 add_add_fusion
  150.7 0.0 copy-done.5
  150.7 0.0 copy-start.2
  150.7 0.6 slice_bitcast_fusion
  151.3 0.0 copy-done.4
  151.3 0.6 reshape.51
  151.9 0.0 copy-done.3
  151.9 0.1 reshape.49
  152.0 0.1 copy.15
  152.1 0.8 reshape.50
  152.8 0.0 copy-done.2
  152.8 0.5 reshape.48
  153.3 0.9 add.17
  (1 shorter events, 0.0 us)
Async XLA Ops:
  0.6 0.7 copy-start.7
  2.0 2.2 %copy-start.1 = (f32[1,1,192,768]{3,2,1,0:T(8,128)S(1)}, f32[1,1,192,768]{3,2,1,0:T(8,128)}, u32[]{:S(2)}) copy-start(f32[1,1,192,768]{3,2,1,0:T(8,128)} %param.8) | copy-start | bytes 1769476
  148.1 1.6 %copy-start = (f32[1,1,192,768]{3,2,1,0:T(8,128)S(1)}, f32[1,1,192,768]{3,2,1,0:T(8,128)}, u32[]{:S(2)}) copy-start(f32[1,1,192,768]{3,2,1,0:T(8,128)} %param.7) | copy-start | bytes 1769476
  148.1 1.6 %copy-start.6 = (f32[768]{0:T(1024)S(1)}, f32[768]{0:T(1024)}, u32[]{:S(2)}) copy-start(f32[768]{0:T(1024)} %param.13) | copy-start | bytes 9220
  149.7 0.9 copy-start.5
  149.8 1.5 copy-start.4
  149.8 2.1 %copy-start.3 = (f32[2,54,2,128]{3,2,1,0:T(2,128)S(1)}, f32[2,54,2,128]{3,2,1,0:T(2,128)}, u32[]{:S(2)}) copy-start(f32[2,54,2,128]{3,2,1,0:T(2,128)} %get-tuple-element.15) | copy-start | bytes 331780
  150.7 2.2 %copy-start.2 = (f32[64,9,2,128]{3,2,1,0:T(2,128)S(1)}, f32[64,9,2,128]{3,2,1,0:T(2,128)}, u32[]{:S(2)}) copy-start(f32[64,9,2,128]{3,2,1,0:T(2,128)} %get-tuple-element.13) | copy-start | bytes 1769476

commit v4 on v3

--- a/solution.py
+++ b/solution.py
@@ -67,6 +67,23 @@
     return mm(a[0], b[0], ca, cb) + (mm(a[1], b[0], ca, cb) + mm(a[0], b[1], ca, cb))
 
 
+def wide(pair):
+    return jnp.concatenate(pair, axis=1)
+
+
+def twice(pair):
+    both = wide(pair)
+    return jnp.concatenate([both, both], axis=0)
+
+
+def tall(pair):
+    return jnp.concatenate([wide((v, v)) for v in pair], axis=0)
+
+
+def halves(r):
+    return r[:, :LANES] + r[:, LANES:]
+
+
 def stacked(left, v):
     return jnp.concatenate([jnp.where(left, v, 0.0), jnp.where(left, 0.0, v)], axis=0)
 
@@ -82,10 +99,10 @@
 
 
 def layer_kernel(
-    x_ref, dy_ref, wq_raw, wp_raw, vec_ref, of, df, rq, rp, so,
-    wq_own, wp_own, x2, dy2, wq2, wp2,
-    xhat, rstd, nh, nl, yh, yl, wh, wl, ph, plo, qkv, da, ah, al, dh, dl, o2, d2, gq2, gp2, sm,
-    ob, db, r1q, r1p, r2q, r2p, aq, ap, hq, hp, fq, fp, zq, zp, eq, ep, es, smx, smy, smz,
+    x_raw, dy_raw, wq_raw, wp_raw, gain_ref, bias_ref, pbias_ref, out, dout, rq, rp, so,
+    xl2, dyl2, of2, df2, eq2, ep2, wq_own, wp_own, x2, dy2, wq2, wp2,
+    xhat, rstd, nh, nl, yh, yl, wh, wl, ph, plo, qkv, da, ah, al, dh, dl, o2, d2, gq2, gp2, sm, pr,
+    ob, db, r1q, r1p, r2q, r2p, aq, ap, hq, hp, fq, fp, zq, zp, es, smx, smy, smz,
     ss, rx, rz, ry, rm, rs, rc, so_sem, rb, r1s, r2s, rh, rf, rzz, ro, ra, re,
 ):
     s, d, z, y, xh, xl, c = position()
@@ -100,6 +117,9 @@
     for n in range(6):
         wp_own[pl.ds(n, 12, stride=6), :] = wp_raw[:, COLS[n]]
     sm[...] = jnp.zeros((24, LANES), F32)
+    x_ref, dy_ref = xl2.reshape(64, 9, 2, LANES), dyl2.reshape(64, 9, 2, LANES)
+    of, df = of2.reshape(64, 9, 2, LANES), df2.reshape(64, 9, 2, LANES)
+    eq, ep = eq2.reshape(4, 54, 2, LANES), ep2.reshape(2, 18, 4, LANES)
     wq_ref, wp_ref = wq_own.reshape(54, 2, LANES), wp_own.reshape(18, 4, LANES)
     xo, dyo = x2.reshape(2, 64, 9, 2, LANES), dy2.reshape(2, 64, 9, 2, LANES)
     o_ref, dx_ref = o2.reshape(2, 64, 9, 2, LANES), d2.reshape(2, 64, 9, 2, LANES)
@@ -113,57 +133,62 @@
     def ydev(k):
         return device((z * 4 + lax.rem(y + k, 4)) * 2 + xh, d)
 
-    def both(j, q_job, p_job):
+    def both(part, j, q_job, p_job):
         at = lax.rem(z + j, 8)
-        q_job(at)
-
-        @pl.when(lax.div(at, 4) == c)
-        def _():
-            p_job(lax.rem(at, 4))
-
-    def along_z(j, to, there, src_q=None, src_p=None):
+        if part == "q":
+            q_job(at)
+        else:
+            @pl.when(lax.div(at, 4) == c)
+            def _():
+                p_job(lax.rem(at, 4))
+
+    def along_z(part, j, to, there, src_q=None, src_p=None):
         both(
+            part,
             j,
             lambda at: send(wqo.at[at, y, xh] if src_q is None else src_q, wqo.at[at, y, xh], ss.at[0], rz.at[0, to], there),
             lambda at: send(wpo.at[at, y, xh] if src_p is None else src_p, wpo.at[at, y, xh], ss.at[1], rz.at[1, to], there),
         )
 
-    def z_stage(j):
+    def z_stage(part, j):
         if j == 0:
-            along_z(0, 7, zdev(1), wq_ref, wp_ref)
-            along_z(0, 1, zdev(-1), wq_ref, wp_ref)
+            along_z(part, 0, 7, zdev(1), wq_ref, wp_ref)
+            along_z(part, 0, 1, zdev(-1), wq_ref, wp_ref)
             both(
+                part,
                 0,
                 lambda at: pltpu.make_async_copy(wq_ref, wqo.at[at, y, xh], rz.at[0, 0]).start(),
                 lambda at: pltpu.make_async_copy(wp_ref, wpo.at[at, y, xh], rz.at[1, 0]).start(),
             )
         both(
+            part,
             j,
             lambda at: wait_for(wqo.at[at, y, xh], rz.at[0, j]),
             lambda at: wait_for(wpo.at[at, y, xh], rz.at[1, j]),
         )
         if j in (7, 6):
-            along_z(j, j - 1, zdev(1))
+            along_z(part, j, j - 1, zdev(1))
         if j in (1, 2):
-            along_z(j, j + 1, zdev(-1))
+            along_z(part, j, j + 1, zdev(-1))
         if j == 5:
             @pl.when(c == 0)
             def _():
-                along_z(5, 4, zdev(1))
+                along_z(part, 5, 4, zdev(1))
         if j == 3:
             @pl.when(c == 1)
             def _():
-                along_z(3, 4, zdev(-1))
-
-    def y_send(j):
+                along_z(part, 3, 4, zdev(-1))
+
+    def y_send(part, j):
         for k in (1, 3):
             both(
+                part,
                 j,
                 lambda at: send(wqo.at[at, y, xh], wqo.at[at, y, xh], ss.at[4], ry.at[0, j, k], ydev(k)),
                 lambda at: send(wpo.at[at, y, xh], wpo.at[at, y, xh], ss.at[5], ry.at[1, j, k], ydev(k)),
             )
 
-    def across(j, k):
+    def across(part, j, k):
         row = lax.rem(y + 4 - k, 4)
         hq, hp = pl.ds(27 * (1 - xl), 27), pl.ds(9 * (1 - xl), 9)
 
@@ -175,17 +200,18 @@
             ref = wpo.at[at, row, xh, hp]
             send(ref, ref, ss.at[7], rm.at[1, j, row], mirror)
 
-        both(j, q, p)
-
-    def y_wait(j, k):
+        both(part, j, q, p)
+
+    def y_wait(part, j, k):
         row = lax.rem(y + 4 - k, 4)
         both(
+            part,
             j,
             lambda at: wait_for(wqo.at[at, row, xh], ry.at[0, j, k]),
             lambda at: wait_for(wpo.at[at, row, xh], ry.at[1, j, k]),
         )
 
-    def y_pass(j, k):
+    def y_pass(part, j, k):
         h = 0 if k == 1 else 1
         row = lax.rem(y + 4 - k, 4)
 
@@ -197,9 +223,9 @@
             ref = wpo.at[at, row, xh, pl.ds(9 * h, 9)]
             send(ref, ref, ss.at[5], ry.at[1, j, 2], ydev(k))
 
-        both(j, q, p)
-
-    def forward(j, k):
+        both(part, j, q, p)
+
+    def forward(part, j, k):
         row = lax.rem(y + 4 - k, 4)
         hq, hp = pl.ds(27 * xl, 27), pl.ds(9 * xl, 9)
 
@@ -213,10 +239,13 @@
             wait_for(ref, rm.at[1, j, row])
             send(ref, ref, ss.at[9], rs.at[1, j, row], side)
 
-        both(j, q, p)
-
-    pltpu.make_async_copy(x_ref.at[s], xo.at[c, s], rx.at[0]).start()
-    pltpu.make_async_copy(dy_ref.at[s], dyo.at[c, s], rx.at[1]).start()
+        both(part, j, q, p)
+
+    def lay_out(n):
+        raw, line, src, dst = ((x_raw, xl2, x_ref, xo), (dy_raw, dyl2, dy_ref, dyo))[n]
+        for i in range(6):
+            line[pl.ds(i, 192, stride=6), :] = raw[:, COLS[i]]
+        pltpu.make_async_copy(src.at[s], dst.at[c, s], rx.at[n]).start()
 
     def spread_in(n, first, last):
         src, dst = ((x_ref, xo), (dy_ref, dyo))[n]
@@ -228,14 +257,16 @@
 
         lax.fori_loop(first, last, one, 0)
 
-    gain = vec_ref[0:1, :]
-    bias = vec_ref[1:2, :]
-
-    def weights(j):
+    gain = gain_ref[...].reshape(1, WIDTH)
+    bias = bias_ref[...].reshape(1, WIDTH)
+    pbias = pbias_ref[...].reshape(1, WIDTH)
+
+    def weights(part, j):
         at = lax.rem(z + j, 8)
         for k in range(4):
             row = lax.rem(y + 4 - k, 4)
             both(
+                part,
                 j,
                 lambda at: wait_for(wqo.at[at, row, 1 - xh, pl.ds(27 * (1 - xl), 27)], rs.at[0, j, row]),
                 lambda at: wait_for(wpo.at[at, row, 1 - xh, pl.ds(9 * (1 - xl), 9)], rs.at[1, j, row]),
@@ -251,7 +282,7 @@
             for n in range(6):
                 ph[rows, COLS[n]], plo[rows, COLS[n]] = split(wp2[pl.ds(at * 576 + n, 96, stride=6), :])
 
-        both(j, q, p)
+        both(part, j, q, p)
 
     def tokens(ref, g):
         base = (g // 3) * 1152 + (g % 3) * 6
@@ -278,38 +309,59 @@
             at = slice(first + n, first + n + 1)
             sm[at, :] = sm[at, :] + v[:, COLS[n]]
 
-    def attention():
-        left = lax.broadcasted_iota(jnp.int32, (LANES, LANES), 1) < 64
-        row = lax.broadcasted_iota(jnp.int32, (2 * LANES, LANES), 0)
-        col = lax.broadcasted_iota(jnp.int32, (2 * LANES, LANES), 1)
-        same = ((row % LANES) < 64) == (col < 64)
-        scale = 0.125
-        for i in range(3):
-            rows = slice(LANES * i, LANES * (i + 1))
-            for h in range(3):
-                q = split(stacked(left, qkv[rows, COLS[h]] * scale))
-                k = split(qkv[rows, COLS[3 + h]])
-                v = split(qkv[rows, COLS[6 + h]])
-                a = split(stacked(left, da[rows, COLS[h]]))
-                scores = jnp.where(same, mm3(q, k, 1, 1), -1e30)
-                e = jnp.exp(scores - jnp.max(scores, axis=1, keepdims=True))
-                probs = e / jnp.sum(e, axis=1, keepdims=True)
-                pair = split(probs)
-                ah[rows, COLS[h]], al[rows, COLS[h]] = split(joined_heads(left, mm3(pair, v, 1, 0)))
-                dh[rows, COLS[6 + h]], dl[rows, COLS[6 + h]] = split(mm3(pair, a, 0, 0))
-                t = mm3(a, v, 1, 1) * probs
-                ds = split(t - probs * jnp.sum(t, axis=1, keepdims=True))
-                dh[rows, COLS[h]], dl[rows, COLS[h]] = split(joined_heads(left, mm3(ds, k, 1, 0)) * scale)
-                dh[rows, COLS[3 + h]], dl[rows, COLS[3 + h]] = split(mm3(ds, q, 0, 0))
+    def query_key_value(t):
+        cols = slice(HALF * t, HALF * (t + 1))
+        qkv[:, cols] = mm3((nh[...], nl[...]), (wh[:, cols], wl[:, cols]), 1, 0)
+
+    def d_attended():
+        da[...] = mm3((yh[...], yl[...]), (ph[...], plo[...]), 1, 1)
+
+    left = lax.broadcasted_iota(jnp.int32, (LANES, LANES), 1) < 64
+    scale = 0.125
+
+    def operands(rows, h):
+        q = wide(split(stacked(left, qkv[rows, COLS[h]] * scale)))
+        return q, split(qkv[rows, COLS[3 + h]]), split(qkv[rows, COLS[6 + h]])
+
+    def forward_attention(i):
+        rows = slice(LANES * i, LANES * (i + 1))
+        first = lax.broadcasted_iota(jnp.int32, (2 * LANES, LANES), 0) % LANES < 64
+        same = first == (lax.broadcasted_iota(jnp.int32, (2 * LANES, LANES), 1) < 64)
+        for h in range(3):
+            q, k, v = operands(rows, h)
+            scores = jnp.where(same, halves(mm(q, tall(k), 1, 1)), -1e30)
+            e = jnp.exp(scores - jnp.max(scores, axis=1, keepdims=True))
+            probs = e / jnp.sum(e, axis=1, keepdims=True)
+            pr[3 * i + h] = probs
+            attended = joined_heads(left, halves(mm(wide(split(probs)), twice(v), 1, 0)))
+            ah[rows, COLS[h]], al[rows, COLS[h]] = split(attended)
+
+    def backward_attention(i):
+        rows = slice(LANES * i, LANES * (i + 1))
+
+        def over_rows(a, b):
+            r = halves(mm(a, b, 0, 0))
+            return r[:LANES] + r[LANES:]
+
+        for h in range(3):
+            q, k, v = operands(rows, h)
+            a = wide(split(stacked(left, da[rows, COLS[h]])))
+            probs = pr[3 * i + h]
+            dh[rows, COLS[6 + h]], dl[rows, COLS[6 + h]] = split(over_rows(wide(split(probs)), a))
+            t = halves(mm(a, tall(v), 1, 1)) * probs
+            ds = wide(split(t - probs * jnp.sum(t, axis=1, keepdims=True)))
+            dq = joined_heads(left, halves(mm(ds, twice(k), 1, 0))) * scale
+            dh[rows, COLS[h]], dl[rows, COLS[h]] = split(dq)
+            dh[rows, COLS[3 + h]], dl[rows, COLS[3 + h]] = split(over_rows(ds, q))
 
     def project(t):
         part = slice(HALF * t, HALF * (t + 1))
         o = mm3((ah[...], al[...]), (ph[:, part], plo[:, part]), 1, 0)
         for g in range(6):
             for n in range(3):
-                o2[pl.ds((g // 3) * 1152 + (g % 3) * 6 + 3 * t + n, 64, stride=18), :] = (
-                    o[64 * g : 64 * (g + 1), COLS[n]]
-                )
+                at = pl.ds((g // 3) * 1152 + (g % 3) * 6 + 3 * t + n, 64, stride=18)
+                own = x2[at, :] + pbias[:, COLS[3 * t + n]]
+                o2[at, :] = o[64 * g : 64 * (g + 1), COLS[n]] + jnp.where(c == g // 3, own, 0.0)
 
     def grad_proj(t):
         part = slice(HALF * t, HALF * (t + 1))
@@ -337,7 +389,8 @@
             m2 = jnp.mean(n * hat, axis=1, keepdims=True)
             dx = rstd[rows, 0:1] * (n - m1 - hat * m2)
             for j in range(6):
-                d2[pl.ds((g // 3) * 1152 + (g % 3) * 6 + j, 64, stride=18), :] = dx[:, COLS[j]]
+                at = pl.ds((g // 3) * 1152 + (g % 3) * 6 + j, 64, stride=18)
+                d2[at, :] = dx[:, COLS[j]] + jnp.where(c == g // 3, dy2[at, :], 0.0)
 
     oxh = 1 - xh
     mine_q, mine_p = pl.ds(27 * xl, 27), pl.ds(9 * xl, 9)
@@ -346,15 +399,16 @@
     def row(k):
         return lax.rem(y + k, 4)
 
-    def side_send(j):
+    def side_send(part, j):
         for k in ROWS:
             both(
+                part,
                 j,
                 lambda at: send(gq_ref.at[at, row(k), oxh, yours_q], r1q.at[j, k], so_sem.at[0], r1s.at[0, j, k], side),
                 lambda at: send(gp_ref.at[at, row(k), oxh, yours_p], r1p.at[j, k], so_sem.at[1], r1s.at[1, j, k], side),
             )
 
-    def mirror_send(j):
+    def mirror_send(part, j):
         for k in ROWS:
             def q(at):
                 wait_for(r1q.at[j, k], r1s.at[0, j, k])
@@ -366,9 +420,9 @@
                 r1p[j, k] = r1p[j, k] + gp_ref[at, row(k), oxh, mine_p]
                 send(r1p.at[j, k], r2p.at[j, k], so_sem.at[6], r2s.at[1, j, k], mirror)
 
-            both(j, q, p)
-
-    def gather(j, k):
+            both(part, j, q, p)
+
+    def gather(part, j, k):
         def q(at):
             wait_for(r2q.at[j, k], r2s.at[0, j, k])
             aq[j, k, mine_q] = gq_ref[at, row(k), xh, mine_q]
@@ -379,37 +433,38 @@
             ap[j, k, mine_p] = gp_ref[at, row(k), xh, mine_p]
             ap[j, k, yours_p] = gp_ref[at, row(k), xh, yours_p] + r2p[j, k]
 
-        both(j, q, p)
-
-    def y_far(j):
-        gather(j, 2)
+        both(part, j, q, p)
+
+    def y_far(part, j):
+        gather(part, j, 2)
         for n, k in ((0, 1), (1, 3)):
             both(
+                part,
                 j,
                 lambda at: send(aq.at[j, 2, pl.ds(27 * n, 27)], hq.at[j, n], so_sem.at[10], rh.at[0, j, n], ydev(k)),
                 lambda at: send(ap.at[j, 2, pl.ds(9 * n, 9)], hp.at[j, n], so_sem.at[11], rh.at[1, j, n], ydev(k)),
             )
 
-    def y_near(j):
+    def y_near(part, j):
         for n, k in ((0, 1), (1, 3)):
-            gather(j, k)
+            gather(part, j, k)
 
             def q(at):
                 wait_for(hq.at[j, n], rh.at[0, j, n])
-                part = pl.ds(27 * n, 27)
-                aq[j, k, part] = aq[j, k, part] + hq[j, n]
+                piece = pl.ds(27 * n, 27)
+                aq[j, k, piece] = aq[j, k, piece] + hq[j, n]
                 send(aq.at[j, k], fq.at[j, n], so_sem.at[10], rf.at[0, j, n], ydev(k))
 
             def p(at):
                 wait_for(hp.at[j, n], rh.at[1, j, n])
-                part = pl.ds(9 * n, 9)
-                ap[j, k, part] = ap[j, k, part] + hp[j, n]
+                piece = pl.ds(9 * n, 9)
+                ap[j, k, piece] = ap[j, k, piece] + hp[j, n]
                 send(ap.at[j, k], fp.at[j, n], so_sem.at[11], rf.at[1, j, n], ydev(k))
 
-            both(j, q, p)
-
-    def z_step(j):
-        gather(j, 0)
+            both(part, j, q, p)
+
+    def z_step(part, j):
+        gather(part, j, 0)
 
         def q(at):
             wait_for(fq.at[j, 0], rf.at[0, j, 0])
@@ -421,7 +476,7 @@
             wait_for(fp.at[j, 1], rf.at[1, j, 1])
             ap[j, 0] = ap[j, 0] + (fp[j, 0] + fp[j, 1])
 
-        both(j, q, p)
+        both(part, j, q, p)
 
         def come(slot):
             def q(at):
@@ -432,10 +487,11 @@
                 wait_for(zp.at[slot], rzz.at[1, slot])
                 ap[j, 0] = ap[j, 0] + zp[slot]
 
-            both(j, q, p)
+            both(part, j, q, p)
 
         def go(slot, k):
             both(
+                part,
                 j,
                 lambda at: send(aq.at[j, 0], zq.at[slot], so_sem.at[13], rzz.at[0, slot], zdev(k)),
                 lambda at: send(ap.at[j, 0], zp.at[slot], so_sem.at[14], rzz.at[1, slot], zdev(k)),
@@ -506,38 +562,70 @@
             for there in (side, mate, corner):
                 send(es.at[d], es.at[d], so_sem.at[17], re.at[2], there)
 
-    for t in range(14):
-        if t < 8:
-            z_stage(ORDER[t])
-            y_send(ORDER[t])
-            across(ORDER[t], 0)
+    def step_in(part, t):
+        if 0 <= t < 8:
+            z_stage(part, ORDER[t])
+            y_send(part, ORDER[t])
+            across(part, ORDER[t], 0)
         if 1 <= t < 9:
             j = ORDER[t - 1]
             for k in (1, 3):
-                y_wait(j, k)
-                y_pass(j, k)
-                across(j, k)
+                y_wait(part, j, k)
+                y_pass(part, j, k)
+                across(part, j, k)
         if 2 <= t < 10:
             j = ORDER[t - 2]
-            y_wait(j, 2)
-            across(j, 2)
-            forward(j, 0)
+            y_wait(part, j, 2)
+            across(part, j, 2)
+            forward(part, j, 0)
         if 3 <= t < 11:
             j = ORDER[t - 3]
             for k in (1, 3, 2):
-                forward(j, k)
-        if 1 <= t <= 4:
-            spread_in(0, 16 * t - 15, min(64, 16 * t + 1))
-        if 5 <= t <= 8:
-            spread_in(1, 16 * t - 79, min(64, 16 * t - 63))
+                forward(part, j, k)
+        if 6 <= t < 14:
+            weights(part, ORDER[t - 6])
+
+    def step_out(part, t):
+        if 0 <= t + 1 < 8:
+            side_send(part, RORDER[t + 1])
+        if 1 <= t < 9:
+            mirror_send(part, RORDER[t - 1])
+        if 2 <= t < 10:
+            y_far(part, RORDER[t - 2])
+        if 3 <= t < 11:
+            y_near(part, RORDER[t - 3])
+        if 4 <= t < 12:
+            z_step(part, RORDER[t - 4])
+
+    for t in range(14):
+        step_in("q", t)
+        step_in("p", t - 0)
+        if t == 0:
+            lay_out(0)
+        if t == 4:
+            lay_out(1)
+        if t == 1:
+            spread_in(0, 1, 16)
+        if t == 2:
+            spread_in(0, 16, 32)
+        if t == 3:
+            spread_in(0, 32, 48)
+        if t == 4:
+            spread_in(0, 48, 64)
+        if t == 5:
+            spread_in(1, 1, 16)
+        if t == 6:
+            spread_in(1, 16, 32)
+        if t == 7:
+            spread_in(1, 32, 48)
+        if t == 8:
+            spread_in(1, 48, 64)
         if t == 10:
             wait_for(xo.at[c], rx.at[0])
             send(xo.at[c], xo.at[c], ss.at[10], rc.at[0], mate)
         if t == 11:
             wait_for(dyo.at[c], rx.at[1])
             send(dyo.at[c], dyo.at[c], ss.at[11], rc.at[1], mate)
-        if 6 <= t < 14:
-            weights(ORDER[t - 6])
         if t == 12:
             wait_for(xo.at[1 - c], rc.at[0])
             for g in range(6):
@@ -546,50 +634,59 @@
             wait_for(dyo.at[1 - c], rc.at[1])
             for g in range(6):
                 cotangent(g)
-
+        if 13 <= t < 13 + 0:
+            query_key_value(t - 13)
+    for t in range(0, 3):
+        query_key_value(t)
+    for i in range(3):
+        forward_attention(i)
+    project(0)
+    project(1)
+    send(o_ref.at[1 - c], ob, so_sem.at[2], rb.at[0], mate)
+    grad_proj(0)
+    grad_proj(1)
+    d_attended()
     for t in range(3):
-        part = slice(HALF * t, HALF * (t + 1))
-        qkv[:, part] = mm3((nh[...], nl[...]), (wh[:, part], wl[:, part]), 1, 0)
-    da[...] = mm3((yh[...], yl[...]), (ph[...], plo[...]), 1, 1)
-    attention()
-    for t in range(3):
-        grad_qkv(t)
-    for t in range(2):
-        grad_proj(t)
-
-    side_send(RORDER[0])
-    side_send(RORDER[1])
-    for t in range(1, 13):
-        if t + 1 < 8:
-            side_send(RORDER[t + 1])
+        backward_attention(t)
+    for n in range(3):
+        grad_qkv(n)
+    for t in range(-1, 12):
+        step_out("p", t)
+        step_out("q", t - 0)
+        if t == 0:
+            joined(0)
         if t == 1:
-            project(0)
-        if 1 <= t < 9:
-            mirror_send(RORDER[t - 1])
+            spread(0, 1, 16)
         if t == 1:
-            project(1)
-            send(o_ref.at[1 - c], ob, so_sem.at[2], rb.at[0], mate)
-        if 2 <= t < 10:
-            y_far(RORDER[t - 2])
-        if t in (2, 3, 4):
-            grad_input(t - 2)
+            spread(0, 16, 32)
+        if t == 1:
+            grad_input(0)
+        if t == 2:
+            spread(0, 32, 48)
+        if t == 2:
+            spread(0, 48, 64)
+        if t == 2:
+            grad_input(1)
+        if t == 3:
+            grad_input(2)
+        if t == 3:
+            send(dx_ref.at[1 - c], db, so_sem.at[3], rb.at[1], mate)
+        if t == 3:
+            small(0)
         if t == 4:
-            send(dx_ref.at[1 - c], db, so_sem.at[3], rb.at[1], mate)
-            small(0)
-        if 3 <= t < 11:
-            y_near(RORDER[t - 3])
-        if 4 <= t < 12:
-            z_step(RORDER[t - 4])
-        if t in (6, 8, 10):
-            small(t // 2 - 2)
-        if t == 2:
-            joined(0)
-        if 2 <= t <= 5:
-            spread(0, 16 * t - 31, min(64, 16 * t - 15))
+            joined(1)
+        if t == 4:
+            spread(1, 1, 22)
         if t == 5:
-            joined(1)
-        if 6 <= t <= 9:
-            spread(1, 16 * t - 95, min(64, 16 * t - 79))
+            spread(1, 22, 43)
+        if t == 5:
+            small(1)
+        if t == 6:
+            spread(1, 43, 64)
+        if t == 7:
+            small(2)
+        if t == 9:
+            small(3)
 
     eq[d] = aq[0, 0]
     for there in (side, mate, corner):
@@ -604,8 +701,12 @@
     wait_for(es.at[pl.ds(0, 3)], re.at[2])
     so[...] = (es[0] + es[2]) + (es[1] + es[3])
     wait_for(eq.at[pl.ds(0, 3)], re.at[0])
-    rq[0] = eq[0] + eq[2]
-    rq[1] = eq[1] + eq[3]
+    for h in range(2):
+        for n in range(9):
+            at = WIDTH * (n // 3) + HALF * h + LANES * (n % 3)
+            rq[:, at : at + LANES] = (
+                eq2[pl.ds(108 * h + n, 12, stride=9), :] + eq2[pl.ds(108 * (h + 2) + n, 12, stride=9), :]
+            )
 
     @pl.when(holds)
     def _():
@@ -615,10 +716,14 @@
     def _():
         wait_for(ep, re.at[1])
 
-    rp[...] = ep[0] + ep[1]
+    for n in range(6):
+        rp[:, COLS[n]] = ep2[pl.ds(n, 12, stride=6), :] + ep2[pl.ds(72 + n, 12, stride=6), :]
 
     wait_for(ob, ro.at[0])
     wait_for(db, ro.at[1])
+    for i in range(6):
+        out[:, COLS[i]] = of2[pl.ds(i, 192, stride=6), :]
+        dout[:, COLS[i]] = df2[pl.ds(i, 192, stride=6), :]
     wait_for(r1q, so_sem.at[0])
     wait_for(r1p.at[pl.ds(0, 4)], so_sem.at[1])
     wait_for(ob, so_sem.at[2])
@@ -666,9 +771,8 @@
     wait_for(xo.at[0], ss.at[11])
 
 
-def layer(x, dy, wq, wp, vectors):
+def layer(x, dy, wq, wp, gain, bias, pbias):
     dma = pltpu.SemaphoreType.DMA
-    anywhere = pl.BlockSpec(memory_space=pl.ANY)
     vmem = pl.BlockSpec(memory_space=pltpu.VMEM)
     act, sml = (64, 9, 2, LANES), (24, LANES)
     q, p = (54, 2, LANES), (18, 4, LANES)
@@ -684,25 +788,26 @@
     return pl.pallas_call(
         layer_kernel,
         out_shape=(
-            jax.ShapeDtypeStruct(act, F32),
-            jax.ShapeDtypeStruct(act, F32),
-            jax.ShapeDtypeStruct((2,) + q, F32),
-            jax.ShapeDtypeStruct(p, F32),
+            jax.ShapeDtypeStruct((192, WIDTH), F32),
+            jax.ShapeDtypeStruct((192, WIDTH), F32),
+            jax.ShapeDtypeStruct((12, 3 * WIDTH), F32),
+            jax.ShapeDtypeStruct((12, WIDTH), F32),
             jax.ShapeDtypeStruct(sml, F32),
         ),
-        in_specs=[anywhere, anywhere, vmem, vmem, vmem],
-        out_specs=(anywhere, anywhere, vmem, vmem, vmem),
+        in_specs=[vmem] * 7,
+        out_specs=(vmem,) * 5,
         scratch_shapes=[
+            buf(1152, LANES), buf(1152, LANES), buf(1152, LANES), buf(1152, LANES), buf(432, LANES), buf(144, LANES),
             buf(108, LANES), buf(72, LANES),
             buf(2304, LANES), buf(2304, LANES), buf(6912, LANES), buf(2304, LANES),
             buf(n, WIDTH), buf(n, LANES), low(n, WIDTH), low(n, WIDTH), low(n, WIDTH), low(n, WIDTH),
             low(WIDTH, 3 * HALF), low(WIDTH, 3 * HALF), low(HALF, WIDTH), low(HALF, WIDTH),
             buf(n, 3 * HALF), buf(n, HALF), low(n, HALF), low(n, HALF), low(n, 3 * HALF), low(n, 3 * HALF),
-            buf(2304, LANES), buf(2304, LANES), buf(6912, LANES), buf(2304, LANES), buf(*sml),
+            buf(2304, LANES), buf(2304, LANES), buf(6912, LANES), buf(2304, LANES), buf(*sml), buf(9, 2 * LANES, LANES),
             buf(*act), buf(*act),
             buf(8, 4, *q2), buf(8, 4, *p2), buf(8, 4, *q2), buf(8, 4, *p2),
             buf(8, 4, *q), buf(8, 4, *p), buf(8, 2, *q2), buf(8, 2, *p2), buf(8, 2, *q), buf(8, 2, *p),
-            buf(9, *q), buf(9, *p), buf(4, *q), buf(2, *p), buf(4, *sml),
+            buf(9, *q), buf(9, *p), buf(4, *sml),
             buf(2, *sml), buf(4, *sml), buf(8, *sml),
             dma((12,)), dma((2,)), dma((2, 8)), dma((2, 8, 4)), dma((2, 8, 4)), dma((2, 8, 4)), dma((2,)),
             dma((18,)), dma((2,)), dma((2, 8, 4)), dma((2, 8, 4)), dma((2, 8, 2)), dma((2, 8, 2)), dma((2, 9)),
@@ -711,29 +816,29 @@
         compiler_params=pltpu.CompilerParams(
             collective_id=0, has_side_effects=True, vmem_limit_bytes=56 * 1024 * 1024
         ),
-    )(x, dy, wq, wp, vectors)
+    )(x, dy, wq, wp, gain, bias, pbias)
 
 
 def on_device(
     frames, out_cotangent, layer_norm_gain, layer_norm_bias, qkv_weight, proj_weight, proj_bias
 ):
-    blocks = (64, 9, 2, LANES)
-    of, df, rq, rp, so = layer(
-        frames.reshape(blocks),
-        out_cotangent.reshape(blocks),
+    out, dout, rq, rp, so = layer(
+        frames.reshape(192, WIDTH),
+        out_cotangent.reshape(192, WIDTH),
         qkv_weight,
         proj_weight,
-        jnp.stack([layer_norm_gain, layer_norm_bias]),
+        layer_norm_gain,
+        layer_norm_bias,
+        proj_bias,
     )
     sums = so[:18].reshape(3, WIDTH)
-    grad_qkv = jnp.transpose(rq.reshape(2, 12, 3, HALF), (1, 2, 0, 3)).reshape(12, 3 * WIDTH)
     return (
-        frames + of.reshape(frames.shape) + proj_bias,
-        out_cotangent + df.reshape(frames.shape),
+        out.reshape(frames.shape),
+        dout.reshape(frames.shape),
         sums[0],
         sums[1],
-        grad_qkv,
-        rp.reshape(12, WIDTH),
+        rq,
+        rp,
         sums[2],
     )
 

time: 155 us -> 146 us (0.942)
  Pallas kernels: 143 us -> 138 us
  local copies, waits for them, and re-layouts: 8.3 us -> 5.73 us
  other arithmetic: 2.36 us -> 0 us
    reshape x7 -> x0, local copies, waits for them, and re-layouts: 6.91 us -> none  [the longest x1 2.23 us: on_device(): frames.reshape(blocks)]
    unnamed x16 -> x12, local copies, waits for them, and re-layouts: 0.04 us -> 5.13 us
    pallas_call x1, Pallas kernels: 143 us -> 138 us  [layer(): pl.pallas_call(layer_kernel, out_shape=(jax.ShapeDtypeStruct((192, WIDTH)...]
    add x2 -> x0, other arithmetic: 1.76 us -> none  [the longest x1 0.88 us: on_device(): frames + of.reshape(frames.shape) + proj_bias]
where the time goes in v4:
time: 146 us; the launch traced here: 144 us
  Pallas kernels  138 us (95%)
  local copies, waits for them, and re-layouts  5.73 us (4%)
    pallas_call x1, Pallas kernels, layer(): pl.pallas_call(layer_kernel, out_shape=(jax.ShapeDtypeStruct((192, WIDTH)...  138 us
    unnamed x12, local copies, waits for them, and re-layouts  5.13 us

profile of v4, /device:TPU:1, one launch (start us, length us, event | category | flops | bytes accessed | tf_op | source)
XLA Modules:
  0.0 144.1 jit_solution(16469233456916358313)
XLA Ops:
  0.6 137.8 %shard_map.126 = (f32[192,768]{1,0:T(8,128)}, f32[192,768]{1,0:T(8,128)}, f32[12,2304]{1,0:T(8,128)}, f32[12,768]{1,0:T(8,128)}, f32[24,128]{1,0:T(8,128)}) custom-call(f32[192,768]{1,0:T(8,128)} %bitcast.12, f32[192,768]{1,0:T(8,128)} %bitcast.13, f32[12,2304]{1,0:T(8,128)} %wq_raw.1, f32[12,768]{1,0:T(8,128)} %wp_raw.1, f32[768]{0:T(1024)} %gain_ref.1, ...), custom_call_target="tpu_custom_call" | custom-call | tf_op jit(solution)/shard_map/pallas_call | solution.py:788
  138.4 0.0 copy-start.3
  138.4 0.7 copy-done.3
  139.1 0.6 slice_bitcast_fusion
  139.7 0.0 copy-start
  139.7 2.0 %copy.18 = f32[1,1,192,768]{3,2,1,0:T(8,128)} copy(f32[1,1,192,768]{3,2,1,0:T(8,128)} %bitcast.11) | data formatting | bytes 1179648
  141.7 0.0 copy-done
  141.7 0.0 copy-start.1
  141.7 0.8 copy.19
  142.5 0.2 copy-done.1
  142.7 0.0 copy-start.2
  142.7 0.7 copy.20
  143.4 0.1 copy-done.2
  143.5 0.6 copy.21
Async XLA Ops:
  138.4 0.7 copy-start.3
  139.7 2.0 %copy-start = (f32[192,768]{1,0:T(8,128)S(1)}, f32[192,768]{1,0:T(8,128)}, u32[]{:S(2)}) copy-start(f32[192,768]{1,0:T(8,128)} %get-tuple-element.13) | copy-start | bytes 1769476
  141.7 1.0 copy-start.1
  142.7 0.8 copy-start.2

commit v5 on v4

--- a/solution.py
+++ b/solution.py
@@ -99,8 +99,8 @@
 
 
 def layer_kernel(
-    x_raw, dy_raw, wq_raw, wp_raw, gain_ref, bias_ref, pbias_ref, out, dout, rq, rp, so,
-    xl2, dyl2, of2, df2, eq2, ep2, wq_own, wp_own, x2, dy2, wq2, wp2,
+    x_hbm, dy_hbm, wq_raw, wp_raw, gain_ref, bias_ref, pbias_ref, out, dout, rq, rp, so,
+    x_raw, dy_raw, fetched, xl2, dyl2, of2, df2, eq2, ep2, wq_own, wp_own, x2, dy2, wq2, wp2,
     xhat, rstd, nh, nl, yh, yl, wh, wl, ph, plo, qkv, da, ah, al, dh, dl, o2, d2, gq2, gp2, sm, pr,
     ob, db, r1q, r1p, r2q, r2p, aq, ap, hq, hp, fq, fp, zq, zp, es, smx, smy, smz,
     ss, rx, rz, ry, rm, rs, rc, so_sem, rb, r1s, r2s, rh, rf, rzz, ro, ra, re,
@@ -109,6 +109,10 @@
     mirror, side, mate = others(s, d, xh, xl, c)
     corner = device(s, (1 - xl) * 2 + 1 - c)
     greet(s, d, (mirror, side, mate, corner))
+    x_fetch = pltpu.make_async_copy(x_hbm, x_raw, fetched.at[0])
+    dy_fetch = pltpu.make_async_copy(dy_hbm, dy_raw, fetched.at[1])
+    x_fetch.start()
+    dy_fetch.start()
     holds = lax.div(z, 4) == c
     for t in range(3):
         for n in range(3):
@@ -243,6 +247,7 @@
 
     def lay_out(n):
         raw, line, src, dst = ((x_raw, xl2, x_ref, xo), (dy_raw, dyl2, dy_ref, dyo))[n]
+        (x_fetch, dy_fetch)[n].wait()
         for i in range(6):
             line[pl.ds(i, 192, stride=6), :] = raw[:, COLS[i]]
         pltpu.make_async_copy(src.at[s], dst.at[c, s], rx.at[n]).start()
@@ -588,18 +593,18 @@
     def step_out(part, t):
         if 0 <= t + 1 < 8:
             side_send(part, RORDER[t + 1])
+        if 0 <= t < 8:
+            mirror_send(part, RORDER[t - 0])
         if 1 <= t < 9:
-            mirror_send(part, RORDER[t - 1])
+            y_far(part, RORDER[t - 1])
         if 2 <= t < 10:
-            y_far(part, RORDER[t - 2])
+            y_near(part, RORDER[t - 2])
         if 3 <= t < 11:
-            y_near(part, RORDER[t - 3])
-        if 4 <= t < 12:
-            z_step(part, RORDER[t - 4])
+            z_step(part, RORDER[t - 3])
 
     for t in range(14):
         step_in("q", t)
-        step_in("p", t - 0)
+        step_in("p", t)
         if t == 0:
             lay_out(0)
         if t == 4:
@@ -650,9 +655,9 @@
         backward_attention(t)
     for n in range(3):
         grad_qkv(n)
-    for t in range(-1, 12):
+    for t in range(-1, 11):
         step_out("p", t)
-        step_out("q", t - 0)
+        step_out("q", t)
         if t == 0:
             joined(0)
         if t == 1:
@@ -687,6 +692,10 @@
             small(2)
         if t == 9:
             small(3)
+        if t == 9:
+            wait_for(ob, ro.at[0])
+            for i in range(6):
+                out[:, COLS[i]] = of2[pl.ds(i, 192, stride=6), :]
 
     eq[d] = aq[0, 0]
     for there in (side, mate, corner):
@@ -719,10 +728,8 @@
     for n in range(6):
         rp[:, COLS[n]] = ep2[pl.ds(n, 12, stride=6), :] + ep2[pl.ds(72 + n, 12, stride=6), :]
 
-    wait_for(ob, ro.at[0])
     wait_for(db, ro.at[1])
     for i in range(6):
-        out[:, COLS[i]] = of2[pl.ds(i, 192, stride=6), :]
         dout[:, COLS[i]] = df2[pl.ds(i, 192, stride=6), :]
     wait_for(r1q, so_sem.at[0])
     wait_for(r1p.at[pl.ds(0, 4)], so_sem.at[1])
@@ -794,9 +801,10 @@
             jax.ShapeDtypeStruct((12, WIDTH), F32),
             jax.ShapeDtypeStruct(sml, F32),
         ),
-        in_specs=[vmem] * 7,
+        in_specs=[pl.BlockSpec(memory_space=pl.ANY)] * 2 + [vmem] * 5,
         out_specs=(vmem,) * 5,
         scratch_shapes=[
+            buf(192, WIDTH), buf(192, WIDTH), dma((2,)),
             buf(1152, LANES), buf(1152, LANES), buf(1152, LANES), buf(1152, LANES), buf(432, LANES), buf(144, LANES),
             buf(108, LANES), buf(72, LANES),
             buf(2304, LANES), buf(2304, LANES), buf(6912, LANES), buf(2304, LANES),

time: 146 us -> 145 us (level)
  no operation moved by 1% of the time
where the time goes in v5:
time: 145 us
  Pallas kernels  138 us (95%)
  local copies, waits for them, and re-layouts  5.73 us (4%)
    pallas_call x1, Pallas kernels, layer(): pl.pallas_call(layer_kernel, out_shape=(jax.ShapeDtypeStruct((192, WIDTH)...  138 us
    unnamed x12, local copies, waits for them, and re-layouts  5.13 us

profile of v5, /device:TPU:1, one launch (start us, length us, event | category | flops | bytes accessed | tf_op | source)
XLA Modules:
  0.0 144.5 jit_solution(2992213132276342077)
XLA Ops:
  0.6 138.1 %shard_map.126 = (f32[192,768]{1,0:T(8,128)}, f32[192,768]{1,0:T(8,128)}, f32[12,2304]{1,0:T(8,128)}, f32[12,768]{1,0:T(8,128)}, f32[24,128]{1,0:T(8,128)}) custom-call(f32[192,768]{1,0:T(8,128)} %bitcast.12, f32[192,768]{1,0:T(8,128)} %bitcast.13, f32[12,2304]{1,0:T(8,128)} %wq_raw.1, f32[12,768]{1,0:T(8,128)} %wp_raw.1, f32[768]{0:T(1024)} %gain_ref.1, ...), custom_call_target="tpu_custom_call" | custom-call | tf_op jit(solution)/shard_map/pallas_call | solution.py:795
  138.8 0.0 copy-start.3
  138.8 0.7 copy-done.3
  139.5 0.6 slice_bitcast_fusion
  140.1 0.0 copy-start
  140.1 2.0 %copy.18 = f32[1,1,192,768]{3,2,1,0:T(8,128)} copy(f32[1,1,192,768]{3,2,1,0:T(8,128)} %bitcast.11) | data formatting | bytes 1179648
  142.1 0.0 copy-done
  142.1 0.0 copy-start.1
  142.1 0.8 copy.19
  142.9 0.2 copy-done.1
  143.1 0.0 copy-start.2
  143.1 0.7 copy.20
  143.8 0.1 copy-done.2
  143.9 0.6 copy.21
Async XLA Ops:
  138.8 0.7 copy-start.3
  140.1 2.0 %copy-start = (f32[192,768]{1,0:T(8,128)S(1)}, f32[192,768]{1,0:T(8,128)}, u32[]{:S(2)}) copy-start(f32[192,768]{1,0:T(8,128)} %get-tuple-element.13) | copy-start | bytes 1769476
  142.1 1.0 copy-start.1
  143.1 0.8 copy-start.2
